TPU v7x, 256 devices: a whole 4x4x8 slice. The times are simulated.
256 devices in a mesh: row: 2 (over x_lo), pass: 64 (over y, z, core), span: 2 (over x_hi).
Axes of the slice: x: 4 (x_hi: 2, x_lo: 2; x = x_hi * 2 + x_lo), y: 4, z: 8, core: 2. Of those that a mesh axis runs over, the one named last changes fastest.
Arguments:
- state: float32 [2, 5, 125, 1, 8, 8192], P('row', None, None, None, 'span', 'pass'), may hold values from -6 to 6
- old_state: float32 [2, 5, 125, 1, 8, 8192], P('row', None, None, None, 'span', 'pass'), may hold values from -6 to 6
- jacobians: float32 [3, 5, 5], replicated, may hold values from -2.5 to 2.5
- offset: int32 [1], replicated, may hold values from 0 to 8191
Outputs:
- residual: float32 [2, 5, 125, 1, 8, 8192], P('row', None, None, None, 'span', 'pass')
- correction: float32 [2, 5, 125, 1, 8, 8192], P('row', None, None, None, 'span', 'pass')
Inputs may be any that keep to these rules, and one draw needn't show every extreme that they name: The offset is a whole number of pitchwise elements.
All inputs are finite; a program needn't handle non-finite values.
Results may differ from a plain program's by a relative error of at most 0.00011.
Values sent between devices are 32-bit elements; how exact they have to be, the bound alone decides.
A program may use at most 192 MiB of HBM per device.

v0:
```python
import math

import jax
import jax.numpy as jnp
import numpy as np
from jax import lax
from jax.sharding import PartitionSpec as P

SWEEPS = 3


LIFT_HALF = 5.0
INV_DT = 1.5
INV_DTAU = 1.0
DIAG = 12.0
OMEGA = 0.7


def from_partner(block, axis, apart):
    count = lax.axis_size(axis)
    route = []
    for low in range(count):
        high = low | 1 << apart
        if high != low and high < count:
            route += [(low, high), (high, low)]
    return lax.ppermute(block, axis, route)


def from_behind(block, axis, distance):
    devices = range(lax.axis_size(axis))
    route = [((i - distance) % len(devices), i) for i in devices]
    return lax.ppermute(block, axis, route)


def extended_2(x, sides, width):
    for axis, dim in sides:
        size, length = (lax.axis_size(axis), x.shape[dim])
        up = [(i, (i + 1) % size) for i in range(size)]
        down = [(j, i) for i, j in up]
        last = lax.slice_in_dim(x, length - width, length, axis=dim)
        first = lax.slice_in_dim(x, 0, width, axis=dim)
        before = lax.ppermute(last, axis, up)
        after = lax.ppermute(first, axis, down)
        x = jnp.concatenate([before, x, after], axis=dim)
    return x


def gll_derivative():
    nodes = np.array([-1.0, -math.sqrt(3.0 / 7.0), 0.0, math.sqrt(3.0 / 7.0), 1.0])
    legend = (35.0 * nodes**4 - 30.0 * nodes**2 + 3.0) / 8.0
    table = np.zeros((5, 5))
    for left in range(5):
        for right in range(5):
            if left != right:
                table[left, right] = legend[left] / (legend[right] * (nodes[left] - nodes[right]))
    table[0, 0] = -5.0
    table[4, 4] = 5.0
    return jnp.asarray(table, jnp.float32)


def face_term(matrix, sign, jump):
    mixed = jnp.einsum("wv,v...->w...", matrix, jump, precision=lax.Precision.HIGHEST)
    return LIFT_HALF * (sign * mixed - jump)


def apply_core(core, jacobians, lo_trace, hi_trace, pitch_lo, pitch_hi, span_lo, span_hi):
    highest = lax.Precision.HIGHEST
    deriv = gll_derivative()
    grad_a = jnp.einsum("ij,vjbcxyz->vibcxyz", deriv, core, precision=highest)
    grad_p = jnp.einsum("ij,vajcxyz->vaicxyz", deriv, core, precision=highest)
    grad_s = jnp.einsum("ij,vabjxyz->vabixyz", deriv, core, precision=highest)
    result = jnp.einsum("wv,vabcxyz->wabcxyz", jacobians[0], grad_a, precision=highest)
    result = result + jnp.einsum("wv,vabcxyz->wabcxyz", jacobians[1], grad_p, precision=highest)
    result = result + jnp.einsum("wv,vabcxyz->wabcxyz", jacobians[2], grad_s, precision=highest)
    in_lo = core[:, 0]
    in_hi = core[:, 4]
    out_lo = jnp.concatenate([lo_trace[:, :, :, None], in_hi[:, :, :, :-1]], axis=3)
    out_hi = jnp.concatenate([in_lo[:, :, :, 1:], hi_trace[:, :, :, None]], axis=3)
    result = result.at[:, 0].add(face_term(jacobians[0], -1.0, out_lo - in_lo))
    result = result.at[:, 4].add(face_term(jacobians[0], 1.0, out_hi - in_hi))
    in_lo = core[:, :, 0]
    in_hi = core[:, :, 4]
    result = result.at[:, :, 0].add(face_term(jacobians[1], -1.0, pitch_lo - in_lo))
    result = result.at[:, :, 4].add(face_term(jacobians[1], 1.0, pitch_hi - in_hi))
    in_lo = core[:, :, :, 0]
    in_hi = core[:, :, :, 4]
    result = result.at[:, :, :, 0].add(face_term(jacobians[2], -1.0, span_lo - in_lo))
    result = result.at[:, :, :, 4].add(face_term(jacobians[2], 1.0, span_hi - in_hi))
    return result


def apply_op(padded, jacobians, lo_trace, hi_trace):
    core = padded[..., 1:-1, 1:-1]
    return apply_core(
        core,
        jacobians,
        lo_trace,
        hi_trace,
        padded[:, :, 4, :, :, 1:-1, :-2],
        padded[:, :, 0, :, :, 1:-1, 2:],
        padded[:, :, :, 4, :, :-2, 1:-1],
        padded[:, :, :, 0, :, 2:, 1:-1],
    )


def seal_walls(extended, width, span_pos, span_count):
    places = jnp.arange(extended.shape[5])[:, None]
    lower = jnp.logical_and(span_pos == 0, places < width)
    upper = jnp.logical_and(span_pos == span_count - 1, places >= extended.shape[5] - width)
    keep = jnp.logical_not(jnp.logical_or(lower, upper)).astype(extended.dtype)
    return extended * keep


def per_device(state, old_state, jacobians, offset):
    elem_a = state.shape[3]
    elem_s = state.shape[4]
    elem_p = state.shape[5]
    shape = (5, 5, 5, 5, elem_a, elem_s, elem_p)
    field = state.reshape(shape)
    older = old_state.reshape(shape)
    row_pos = lax.axis_index("row")
    pass_count = lax.axis_size("pass")
    span_count = lax.axis_size("span")
    span_pos = lax.axis_index("span")
    annulus_total = elem_p * pass_count
    mine = jnp.where(row_pos == 0, field[:, 4, :, :, elem_a - 1], field[:, 0, :, :, 0])
    other = from_partner(mine, "row", 0)
    turned = offset[0] % annulus_total
    amount = jnp.where(row_pos == 0, (annulus_total - turned) % annulus_total, turned)
    passages = amount // elem_p
    within = amount % elem_p
    moved = other
    for digit in range((pass_count - 1).bit_length()):
        arrived = from_behind(moved, "pass", 1 << digit)
        moved = jnp.where((passages >> digit) % 2 == 1, arrived, moved)
    before = from_behind(moved, "pass", 1)
    joined = jnp.concatenate([before, moved], axis=4)
    facing = lax.dynamic_slice_in_dim(joined, elem_p - within, elem_p, 4)
    blank = jnp.zeros_like(facing)
    lower = jnp.where(row_pos == 0, blank, facing)
    upper = jnp.where(row_pos == 0, facing, blank)
    padded = extended_2(field, (("pass", 6), ("span", 5)), 1)
    padded = seal_walls(padded, 1, span_pos, span_count)
    operated = apply_op(padded, jacobians, lower, upper)
    residual = (field - older) * INV_DT + operated
    rate = OMEGA / DIAG
    update = -residual / DIAG
    for sweep in range(SWEEPS):
        extended = extended_2(update, (("pass", 6), ("span", 5)), 1)
        extended = seal_walls(extended, 1, span_pos, span_count)
        swept = apply_op(extended, jacobians, blank, blank)
        image = (INV_DT + INV_DTAU) * update + swept
        update = update - rate * (residual + image)
    final = (1, 5, 125, elem_a, elem_s, elem_p)
    return (residual.reshape(final), update.reshape(final))


def solution(mesh):
    placed = (
        P("row", None, None, None, "span", "pass"),
        P("row", None, None, None, "span", "pass"),
        P(),
        P(),
    )
    return jax.shard_map(
        per_device,
        mesh=mesh,
        in_specs=placed,
        out_specs=(
            P("row", None, None, None, "span", "pass"),
            P("row", None, None, None, "span", "pass"),
        ),
        check_vma=False,
    )
```

profile of v0, /device:TPU:4, one launch (start us, length us, event | category | flops | bytes accessed | tf_op | source)
XLA Modules:
  0.0 539.4 jit_solution(8038844690608227472)
XLA Ops:
  0.6 3.5 fusion.225
  4.2 5.1 copy.350
  9.3 7.7 %collective-permute-start.1 = (f32[5,5,5,5,1,4,1]{3,5,6,4,2,1,0:T(4,128)}, f32[5,5,5,5,1,4,1]{3,5,6,4,2,1,0:T(4,128)}, u32[]{:S(2)}, u32[]{:S(2)}) collective-permute-start(f32[5,5,5,5,1,4,1]{3,5,6,4,2,1,0:T(4,128)} %copy.350), channel_id=1, source_target_pairs={{2,0},{4,2},{6,4},{8,6},{10,8},{12,10},{14,12},{16,14},{18,16},{20... | collective-permute-start | bytes 30008 | tf_op jit(solution)/shard_map/ppermute | solution.py:43
  17.0 3.7 copy.349
  23.1 8.0 %copy.353 = f32[5,5,5,5,1,4,1]{6,1,5,3,2,0,4:T(8,128)} copy(f32[5,5,5,5,1,4,1]{3,5,6,4,2,1,0:T(4,128)} %collective-permute-done.1) | data formatting | bytes 20000 | tf_op jit(solution)/shard_map/ppermute | solution.py:43
  31.1 8.0 %copy.351 = f32[5,5,5,5,1,4,1]{6,1,5,3,2,0,4:T(8,128)} copy(f32[5,5,5,5,1,4,1]{3,5,6,4,2,1,0:T(4,128)} %collective-permute-done) | data formatting | bytes 20000 | tf_op jit(solution)/shard_map/ppermute | solution.py:42
  49.2 13.0 %collective-permute-done.3 = f32[5,5,5,5,1,1,130]{6,5,4,3,2,1,0:T(1,128)} collective-permute-done((f32[5,5,5,5,1,1,130]{6,5,4,3,2,1,0:T(1,128)}, f32[5,5,5,5,1,1,130]{6,5,4,3,2,1,0:T(1,128)}, u32[]{:S(2)}, u32[]{:S(2)}) %collective-permute-start.3) | collective-permute-done | bytes 325032 | tf_op jit(solution)/shard_map/ppermute | solution.py:43
  63.4 5.6 %collective-permute-done.2 = f32[5,5,5,5,1,1,130]{6,5,4,3,2,1,0:T(1,128)} collective-permute-done((f32[5,5,5,5,1,1,130]{6,5,4,3,2,1,0:T(1,128)}, f32[5,5,5,5,1,1,130]{6,5,4,3,2,1,0:T(1,128)}, u32[]{:S(2)}, u32[]{:S(2)}) %collective-permute-start.2) | collective-permute-done | bytes 325032 | tf_op jit(solution)/shard_map/ppermute | solution.py:42
  70.3 5.0 maximum_multiply_fusion
  96.4 8.0 %collective-permute-done.6 = f32[5,5,5,4,128]{4,3,0,1,2:T(4,128)S(1)} collective-permute-done((f32[5,5,5,4,128]{4,3,0,1,2:T(4,128)S(1)}, f32[5,5,5,4,128]{4,3,0,1,2:T(4,128)S(1)}, u32[]{:S(2)}, u32[]{:S(2)}) %collective-permute-start.6) | collective-permute-done | bytes 256032 | tf_op jit(solution)/shard_map/ppermute | solution.py:32
  105.4 17.3 %collective-permute-done.7 = f32[5,5,5,4,128]{4,3,0,1,2:T(4,128)S(1)} collective-permute-done((f32[5,5,5,4,128]{4,3,0,1,2:T(4,128)S(1)}, f32[5,5,5,4,128]{4,3,0,1,2:T(4,128)S(1)}, u32[]{:S(2)}, u32[]{:S(2)}) %collective-permute-start.7) | collective-permute-done | bytes 256032 | tf_op jit(solution)/shard_map/ppermute | solution.py:32
  124.2 15.9 %collective-permute-done.8 = f32[5,5,5,4,128]{4,3,0,1,2:T(4,128)S(1)} collective-permute-done((f32[5,5,5,4,128]{4,3,0,1,2:T(4,128)S(1)}, f32[5,5,5,4,128]{4,3,0,1,2:T(4,128)S(1)}, u32[]{:S(2)}, u32[]{:S(2)}) %collective-permute-start.8) | collective-permute-done | bytes 256032 | tf_op jit(solution)/shard_map/ppermute | solution.py:32
  143.4 6.6 %collective-permute-done.9 = f32[5,5,5,4,128]{4,3,0,1,2:T(4,128)S(1)} collective-permute-done((f32[5,5,5,4,128]{4,3,0,1,2:T(4,128)S(1)}, f32[5,5,5,4,128]{4,3,0,1,2:T(4,128)S(1)}, u32[]{:S(2)}, u32[]{:S(2)}) %collective-permute-start.9) | collective-permute-done | bytes 256032 | tf_op jit(solution)/shard_map/ppermute | solution.py:32
  150.8 8.2 %collective-permute-done.10 = f32[5,5,5,4,128]{4,3,0,1,2:T(4,128)S(1)} collective-permute-done((f32[5,5,5,4,128]{4,3,0,1,2:T(4,128)S(1)}, f32[5,5,5,4,128]{4,3,0,1,2:T(4,128)S(1)}, u32[]{:S(2)}, u32[]{:S(2)}) %collective-permute-start.10) | collective-permute-done | bytes 256032 | tf_op jit(solution)/shard_map/ppermute | solution.py:32
  161.9 6.3 %collective-permute-done.11 = f32[5,5,5,4,128]{4,3,0,1,2:T(4,128)S(1)} collective-permute-done((f32[5,5,5,4,128]{4,3,0,1,2:T(4,128)S(1)}, f32[5,5,5,4,128]{4,3,0,1,2:T(4,128)S(1)}, u32[]{:S(2)}, u32[]{:S(2)}) %collective-permute-start.11) | collective-permute-done | bytes 256032 | tf_op jit(solution)/shard_map/ppermute | solution.py:32
  171.4 13.4 %scatter-add.81 = f32[5,5,5,5,1,4,128]{6,1,5,0,2,4,3:T(8,128)S(1)} dynamic-update-slice(f32[5,5,5,5,1,4,128]{6,1,5,0,2,4,3:T(8,128)S(1)} %copy.383, f32[5,1,5,5,1,4,128]{6,1,5,0,2,4,3:T(1,128)} %add.306, s32[]{:T(128)} %constant.604.clone.1, s32[]{:T(128)} %constant.615.clone.1, s32[]{:T(128)} %constant.604.clone.1, s32[]{:T(128)} %constant.604.clone.1, s32[]{:T(128)} %constant.604.clone.1, ...) | dynamic-update-slice | bytes 512004 | tf_op jit(solution)/shard_map/scatter-add | solution.py:80
  194.4 4.7 copy.406
  199.3 4.7 copy.405
  204.6 7.1 %copy.408 = f32[5,5,5,5,1,4,1]{6,2,5,0,3,4,1:T(8,128)} copy(f32[5,5,5,5,1,4,1]{3,5,6,4,2,1,0:T(4,128)S(1)} %collective-permute-done.13) | data formatting | bytes 20000 | tf_op jit(solution)/shard_map/ppermute | solution.py:43
  213.1 7.1 %copy.407 = f32[5,5,5,5,1,4,1]{6,2,5,0,3,4,1:T(8,128)} copy(f32[5,5,5,5,1,4,1]{3,5,6,4,2,1,0:T(4,128)S(1)} %collective-permute-done.12) | data formatting | bytes 20000 | tf_op jit(solution)/shard_map/ppermute | solution.py:42
  225.1 2.8 collective-permute-start.14
  228.0 14.6 %collective-permute-done.15 = f32[5,5,5,5,1,1,130]{6,5,4,3,2,1,0:T(1,128)S(1)} collective-permute-done((f32[5,5,5,5,1,1,130]{6,5,4,3,2,1,0:T(1,128)S(1)}, f32[5,5,5,5,1,1,130]{6,5,4,3,2,1,0:T(1,128)S(1)}, u32[]{:S(2)}, u32[]{:S(2)}) %collective-permute-start.15) | collective-permute-done | bytes 325032 | tf_op jit(solution)/shard_map/ppermute | solution.py:43
  242.7 11.1 %collective-permute-done.14 = f32[5,5,5,5,1,1,130]{6,5,4,3,2,1,0:T(1,128)S(1)} collective-permute-done((f32[5,5,5,5,1,1,130]{6,5,4,3,2,1,0:T(1,128)S(1)}, f32[5,5,5,5,1,1,130]{6,5,4,3,2,1,0:T(1,128)S(1)}, u32[]{:S(2)}, u32[]{:S(2)}) %collective-permute-start.14) | collective-permute-done | bytes 325032 | tf_op jit(solution)/shard_map/ppermute | solution.py:42
  254.0 3.8 maximum_multiply_fusion.1
  276.3 3.6 fusion.211
  284.5 10.1 %scatter-add.94 = f32[5,5,5,5,1,4,128]{6,2,5,0,3,4,1:T(8,128)} dynamic-update-slice(f32[5,5,5,5,1,4,128]{6,2,5,0,3,4,1:T(8,128)} %copy-done.17, f32[5,5,1,5,1,4,128]{6,2,5,0,3,4,1:T(1,128)} %bitcast.572, s32[]{:T(128)} %constant.604.clone.1, s32[]{:T(128)} %constant.604.clone.1, s32[]{:T(128)} %constant.604.clone.1, s32[]{:T(128)} %constant.604.clone.1, s32[]{:T(128)} %constant.604.clone.1, ...) | dynamic-update-slice | bytes 512004 | tf_op jit(solution)/shard_map/scatter-add | solution.py:83
  297.8 10.1 %scatter-add.95 = f32[5,5,5,5,1,4,128]{6,2,5,0,3,4,1:T(8,128)} dynamic-update-slice(f32[5,5,5,5,1,4,128]{6,2,5,0,3,4,1:T(8,128)} %scatter-add.94, f32[5,5,1,5,1,4,128]{6,2,5,0,3,4,1:T(1,128)} %bitcast.573, s32[]{:T(128)} %constant.604.clone.1, s32[]{:T(128)} %constant.604.clone.1, s32[]{:T(128)} %constant.615.clone.1, s32[]{:T(128)} %constant.604.clone.1, s32[]{:T(128)} %constant.604.clone.1, ...) | dynamic-update-slice | bytes 512004 | tf_op jit(solution)/shard_map/scatter-add | solution.py:84
  313.2 2.8 add_add_fusion
  321.1 4.7 copy.455
  326.0 4.7 copy.454
  331.2 7.1 %copy.457 = f32[5,5,5,5,1,4,1]{6,1,5,2,0,4,3:T(8,128)} copy(f32[5,5,5,5,1,4,1]{3,5,6,4,2,1,0:T(4,128)S(1)} %collective-permute-done.17) | data formatting | bytes 20000 | tf_op jit(solution)/shard_map/ppermute | solution.py:43
  339.8 7.1 %copy.456 = f32[5,5,5,5,1,4,1]{6,1,5,2,0,4,3:T(8,128)} copy(f32[5,5,5,5,1,4,1]{3,5,6,4,2,1,0:T(4,128)S(1)} %collective-permute-done.16) | data formatting | bytes 20000 | tf_op jit(solution)/shard_map/ppermute | solution.py:42
  351.8 2.8 collective-permute-start.18
  354.7 14.6 %collective-permute-done.19 = f32[5,5,5,5,1,1,130]{6,5,4,3,2,1,0:T(1,128)S(1)} collective-permute-done((f32[5,5,5,5,1,1,130]{6,5,4,3,2,1,0:T(1,128)S(1)}, f32[5,5,5,5,1,1,130]{6,5,4,3,2,1,0:T(1,128)S(1)}, u32[]{:S(2)}, u32[]{:S(2)}) %collective-permute-start.19) | collective-permute-done | bytes 325032 | tf_op jit(solution)/shard_map/ppermute | solution.py:43
  369.3 11.1 %collective-permute-done.18 = f32[5,5,5,5,1,1,130]{6,5,4,3,2,1,0:T(1,128)S(1)} collective-permute-done((f32[5,5,5,5,1,1,130]{6,5,4,3,2,1,0:T(1,128)S(1)}, f32[5,5,5,5,1,1,130]{6,5,4,3,2,1,0:T(1,128)S(1)}, u32[]{:S(2)}, u32[]{:S(2)}) %collective-permute-start.18) | collective-permute-done | bytes 325032 | tf_op jit(solution)/shard_map/ppermute | solution.py:42
  380.6 3.8 maximum_multiply_fusion.2
  403.6 3.6 fusion.213
  410.4 10.1 %scatter-add.104 = f32[5,5,5,5,1,4,128]{6,2,5,0,3,4,1:T(8,128)} dynamic-update-slice(f32[5,5,5,5,1,4,128]{6,2,5,0,3,4,1:T(8,128)} %copy-done.18, f32[5,5,1,5,1,4,128]{6,2,5,0,3,4,1:T(1,128)} %slice_add_fusion.12, s32[]{:T(128)} %constant.604.clone.1, s32[]{:T(128)} %constant.604.clone.1, s32[]{:T(128)} %constant.604.clone.1, s32[]{:T(128)} %constant.604.clone.1, s32[]{:T(128)} %constant.604.clone.1, ...) | dynamic-update-slice | bytes 512004 | tf_op jit(solution)/shard_map/scatter-add | solution.py:83
  423.1 10.1 %scatter-add.105 = f32[5,5,5,5,1,4,128]{6,2,5,0,3,4,1:T(8,128)} dynamic-update-slice(f32[5,5,5,5,1,4,128]{6,2,5,0,3,4,1:T(8,128)} %scatter-add.104, f32[5,5,1,5,1,4,128]{6,2,5,0,3,4,1:T(1,128)S(1)} %slice_add_fusion.11, s32[]{:T(128)} %constant.604.clone.1, s32[]{:T(128)} %constant.604.clone.1, s32[]{:T(128)} %constant.615.clone.1, s32[]{:T(128)} %constant.604.clone.1, s32[]{:T(128)} %constant.604.clone.1, ...) | dynamic-update-slice | bytes 512004 | tf_op jit(solution)/shard_map/scatter-add | solution.py:84
  445.1 4.7 copy.502
  450.2 4.7 copy.501
  455.4 7.1 %copy.504 = f32[5,5,5,5,1,4,1]{6,1,5,2,0,4,3:T(8,128)} copy(f32[5,5,5,5,1,4,1]{3,5,6,4,2,1,0:T(4,128)S(1)} %collective-permute-done.21) | data formatting | bytes 20000 | tf_op jit(solution)/shard_map/ppermute | solution.py:43
  464.0 7.1 %copy.503 = f32[5,5,5,5,1,4,1]{6,1,5,2,0,4,3:T(8,128)} copy(f32[5,5,5,5,1,4,1]{3,5,6,4,2,1,0:T(4,128)S(1)} %collective-permute-done.20) | data formatting | bytes 20000 | tf_op jit(solution)/shard_map/ppermute | solution.py:42
  476.0 2.8 collective-permute-start.22
  480.2 13.2 %collective-permute-done.23 = f32[5,5,5,5,1,1,130]{6,5,4,3,2,1,0:T(1,128)S(1)} collective-permute-done((f32[5,5,5,5,1,1,130]{6,5,4,3,2,1,0:T(1,128)S(1)}, f32[5,5,5,5,1,1,130]{6,5,4,3,2,1,0:T(1,128)S(1)}, u32[]{:S(2)}, u32[]{:S(2)}) %collective-permute-start.23) | collective-permute-done | bytes 325032 | tf_op jit(solution)/shard_map/ppermute | solution.py:43
  493.5 11.1 %collective-permute-done.22 = f32[5,5,5,5,1,1,130]{6,5,4,3,2,1,0:T(1,128)S(1)} collective-permute-done((f32[5,5,5,5,1,1,130]{6,5,4,3,2,1,0:T(1,128)S(1)}, f32[5,5,5,5,1,1,130]{6,5,4,3,2,1,0:T(1,128)S(1)}, u32[]{:S(2)}, u32[]{:S(2)}) %collective-permute-start.22) | collective-permute-done | bytes 325032 | tf_op jit(solution)/shard_map/ppermute | solution.py:42
  504.8 3.5 maximum_multiply_fusion.3
  526.9 3.6 fusion.215
  (244 shorter events, 181.0 us)
Async XLA Ops:
  4.2 16.6 %copy-start.9 = (f32[1,5,125,1,4,128]{5,4,3,2,1,0:T(4,128)S(1)}, f32[1,5,125,1,4,128]{5,4,3,2,1,0:T(4,128)}, u32[]{:S(2)}) copy-start(f32[1,5,125,1,4,128]{5,4,3,2,1,0:T(4,128)} %param.56) | copy-start | bytes 3840004
  9.3 13.8 %collective-permute-start.1 = (f32[5,5,5,5,1,4,1]{3,5,6,4,2,1,0:T(4,128)}, f32[5,5,5,5,1,4,1]{3,5,6,4,2,1,0:T(4,128)}, u32[]{:S(2)}, u32[]{:S(2)}) collective-permute-start(f32[5,5,5,5,1,4,1]{3,5,6,4,2,1,0:T(4,128)} %copy.350), channel_id=1, source_target_pairs={{2,0},{4,2},{6,4},{8,6},{10,8},{12,10},{14,12},{16,14},{18,16},{20... | collective-permute-start | bytes 30008 | tf_op jit(solution)/shard_map/ppermute | solution.py:43
  20.7 10.4 %collective-permute-start = (f32[5,5,5,5,1,4,1]{3,5,6,4,2,1,0:T(4,128)}, f32[5,5,5,5,1,4,1]{3,5,6,4,2,1,0:T(4,128)}, u32[]{:S(2)}, u32[]{:S(2)}) collective-permute-start(f32[5,5,5,5,1,4,1]{3,5,6,4,2,1,0:T(4,128)} %copy.349), channel_id=1, source_target_pairs={{0,2},{2,4},{4,6},{6,8},{8,10},{10,12},{12,14},{14,16},{16,18},{18... | collective-permute-start | bytes 30008 | tf_op jit(solution)/shard_map/ppermute | solution.py:42
  21.5 27.5 %collective-permute-start.4 = (f32[5,5,5,4,128]{4,3,0,1,2:T(4,128)}, f32[5,5,5,4,128]{4,3,0,1,2:T(4,128)}, u32[]{:S(2)}, u32[]{:S(2)}) collective-permute-start(f32[5,5,5,4,128]{4,3,0,1,2:T(4,128)} %fusion.206), channel_id=1, source_target_pairs={{0,128},{128,0},{1,129},{129,1},{2,130},{130,2},{3,131},{131,3},{4... | collective-permute-start | bytes 768008 | tf_op jit(solution)/shard_map/ppermute | solution.py:26
  41.5 7.5 %copy-start.29 = (f32[3,5,5]{2,0,1:T(4,128)S(1)}, f32[3,5,5]{2,0,1:T(4,128)}, u32[]{:S(2)}) copy-start(f32[3,5,5]{2,0,1:T(4,128)} %param.58) | copy-start | bytes 904
  43.0 19.2 %collective-permute-start.3 = (f32[5,5,5,5,1,1,130]{6,5,4,3,2,1,0:T(1,128)}, f32[5,5,5,5,1,1,130]{6,5,4,3,2,1,0:T(1,128)}, u32[]{:S(2)}, u32[]{:S(2)}) collective-permute-start(f32[5,5,5,5,1,1,130]{6,5,4,3,2,1,0:T(1,128)} %copy.355), channel_id=1, source_target_pairs={{1,0},{0,1},{3,2},{2,3},{5,4},{4,5},{7,6},{6,7},{9,8},{8,9},{11,10... | collective-permute-start | bytes 975008 | tf_op jit(solution)/shard_map/ppermute | solution.py:43
  45.5 23.6 %collective-permute-start.2 = (f32[5,5,5,5,1,1,130]{6,5,4,3,2,1,0:T(1,128)}, f32[5,5,5,5,1,1,130]{6,5,4,3,2,1,0:T(1,128)}, u32[]{:S(2)}, u32[]{:S(2)}) collective-permute-start(f32[5,5,5,5,1,1,130]{6,5,4,3,2,1,0:T(1,128)} %copy.354), channel_id=1, source_target_pairs={{0,1},{1,0},{2,3},{3,2},{4,5},{5,4},{6,7},{7,6},{8,9},{9,8},{10,11... | collective-permute-start | bytes 975008 | tf_op jit(solution)/shard_map/ppermute | solution.py:42
  49.1 21.2 %copy-start.10 = (f32[5,5,5,5,1,4,1]{6,1,5,3,2,0,4:T(8,128)S(1)}, f32[5,5,5,5,1,4,1]{6,1,5,3,2,0,4:T(8,128)}, u32[]{:S(2)}) copy-start(f32[5,5,5,5,1,4,1]{6,1,5,3,2,0,4:T(8,128)} %copy.353) | copy-start | bytes 30004
  49.1 43.7 %collective-permute-start.5 = (f32[5,5,5,4,128]{4,3,0,1,2:T(4,128)}, f32[5,5,5,4,128]{4,3,0,1,2:T(4,128)S(1)}, u32[]{:S(2)}, u32[]{:S(2)}) collective-permute-start(f32[5,5,5,4,128]{4,3,0,1,2:T(4,128)} %collective-permute-done.4), channel_id=1, source_target_pairs={{126,0},{0,2},{2,4},{4,6},{6,8},{8,10},{10,12},{12,14},{14,16},{16... | collective-permute-start | bytes 768008 | tf_op jit(solution)/shard_map/ppermute | solution.py:32
  93.9 10.6 %collective-permute-start.6 = (f32[5,5,5,4,128]{4,3,0,1,2:T(4,128)S(1)}, f32[5,5,5,4,128]{4,3,0,1,2:T(4,128)S(1)}, u32[]{:S(2)}, u32[]{:S(2)}) collective-permute-start(f32[5,5,5,4,128]{4,3,0,1,2:T(4,128)S(1)} %broadcast_select_fusion), channel_id=1, source_target_pairs={{124,0},{126,2},{0,4},{2,6},{4,8},{6,10},{8,12},{10,14},{12,16},{1... | collective-permute-start | bytes 768008 | tf_op jit(solution)/shard_map/ppermute | solution.py:32
  104.5 18.2 %collective-permute-start.7 = (f32[5,5,5,4,128]{4,3,0,1,2:T(4,128)S(1)}, f32[5,5,5,4,128]{4,3,0,1,2:T(4,128)S(1)}, u32[]{:S(2)}, u32[]{:S(2)}) collective-permute-start(f32[5,5,5,4,128]{4,3,0,1,2:T(4,128)S(1)} %broadcast_select_fusion.1), channel_id=1, source_target_pairs={{120,0},{122,2},{124,4},{126,6},{0,8},{2,10},{4,12},{6,14},{8,16},... | collective-permute-start | bytes 768008 | tf_op jit(solution)/shard_map/ppermute | solution.py:32
  122.8 17.3 %collective-permute-start.8 = (f32[5,5,5,4,128]{4,3,0,1,2:T(4,128)S(1)}, f32[5,5,5,4,128]{4,3,0,1,2:T(4,128)S(1)}, u32[]{:S(2)}, u32[]{:S(2)}) collective-permute-start(f32[5,5,5,4,128]{4,3,0,1,2:T(4,128)S(1)} %broadcast_select_fusion.2), channel_id=1, source_target_pairs={{112,0},{114,2},{116,4},{118,6},{120,8},{122,10},{124,12},{126,14}... | collective-permute-start | bytes 768008 | tf_op jit(solution)/shard_map/ppermute | solution.py:32
  124.2 26.5 %copy-start.19 = (f32[5,5,5,4,128]{4,1,3,0,2:T(8,128)}, f32[5,5,5,4,128]{4,1,3,0,2:T(8,128)S(1)}, u32[]{:S(2)}) copy-start(f32[5,5,5,4,128]{4,1,3,0,2:T(8,128)S(1)} %get-tuple-element.354) | copy-start | bytes 768004
  124.2 26.5 %copy-start.20 = (f32[5,5,5,4,128]{4,1,3,0,2:T(8,128)}, f32[5,5,5,4,128]{4,1,3,0,2:T(8,128)S(1)}, u32[]{:S(2)}) copy-start(f32[5,5,5,4,128]{4,1,3,0,2:T(8,128)S(1)} %get-tuple-element.355) | copy-start | bytes 768004
  140.2 9.8 %collective-permute-start.9 = (f32[5,5,5,4,128]{4,3,0,1,2:T(4,128)S(1)}, f32[5,5,5,4,128]{4,3,0,1,2:T(4,128)S(1)}, u32[]{:S(2)}, u32[]{:S(2)}) collective-permute-start(f32[5,5,5,4,128]{4,3,0,1,2:T(4,128)S(1)} %broadcast_select_fusion.3), channel_id=1, source_target_pairs={{96,0},{98,2},{100,4},{102,6},{104,8},{106,10},{108,12},{110,14},{... | collective-permute-start | bytes 768008 | tf_op jit(solution)/shard_map/ppermute | solution.py:32
  150.1 8.9 %collective-permute-start.10 = (f32[5,5,5,4,128]{4,3,0,1,2:T(4,128)S(1)}, f32[5,5,5,4,128]{4,3,0,1,2:T(4,128)S(1)}, u32[]{:S(2)}, u32[]{:S(2)}) collective-permute-start(f32[5,5,5,4,128]{4,3,0,1,2:T(4,128)S(1)} %broadcast_select_fusion.4), channel_id=1, source_target_pairs={{64,0},{66,2},{68,4},{70,6},{72,8},{74,10},{76,12},{78,14},{80,16}... | collective-permute-start | bytes 768008 | tf_op jit(solution)/shard_map/ppermute | solution.py:32
  150.7 18.1 %copy-start.23 = (f32[5,5,5,4,128]{4,1,3,2,0:T(8,128)}, f32[5,5,5,4,128]{4,1,3,2,0:T(8,128)S(1)}, u32[]{:S(2)}) copy-start(f32[5,5,5,4,128]{4,1,3,2,0:T(8,128)S(1)} %get-tuple-element.328) | copy-start | bytes 768004
  150.8 8.4 %copy-start.21 = (f32[5,5,5,4,128]{4,1,3,0,2:T(8,128)}, f32[5,5,5,4,128]{4,1,3,0,2:T(8,128)S(1)}, u32[]{:S(2)}) copy-start(f32[5,5,5,4,128]{4,1,3,0,2:T(8,128)S(1)} %fusion.124) | copy-start | bytes 768004
  159.1 9.1 %collective-permute-start.11 = (f32[5,5,5,4,128]{4,3,0,1,2:T(4,128)S(1)}, f32[5,5,5,4,128]{4,3,0,1,2:T(4,128)S(1)}, u32[]{:S(2)}, u32[]{:S(2)}) collective-permute-start(f32[5,5,5,4,128]{4,3,0,1,2:T(4,128)S(1)} %broadcast_select_fusion.5), channel_id=1, source_target_pairs={{126,0},{0,2},{2,4},{4,6},{6,8},{8,10},{10,12},{12,14},{14,16},{16... | collective-permute-start | bytes 768008 | tf_op jit(solution)/shard_map/ppermute | solution.py:32
  187.7 1.4 copy-start.24
  187.7 1.4 copy-start.25
  191.7 2.7 copy-start.5
  199.1 5.5 %collective-permute-start.13 = (f32[5,5,5,5,1,4,1]{3,5,6,4,2,1,0:T(4,128)S(1)}, f32[5,5,5,5,1,4,1]{3,5,6,4,2,1,0:T(4,128)S(1)}, u32[]{:S(2)}, u32[]{:S(2)}) collective-permute-start(f32[5,5,5,5,1,4,1]{3,5,6,4,2,1,0:T(4,128)S(1)} %copy.406), channel_id=1, source_target_pairs={{2,0},{4,2},{6,4},{8,6},{10,8},{12,10},{14,12},{16,14},{18,16},{20... | collective-permute-start | bytes 30008 | tf_op jit(solution)/shard_map/ppermute | solution.py:43
  204.0 9.1 %collective-permute-start.12 = (f32[5,5,5,5,1,4,1]{3,5,6,4,2,1,0:T(4,128)S(1)}, f32[5,5,5,5,1,4,1]{3,5,6,4,2,1,0:T(4,128)S(1)}, u32[]{:S(2)}, u32[]{:S(2)}) collective-permute-start(f32[5,5,5,5,1,4,1]{3,5,6,4,2,1,0:T(4,128)S(1)} %copy.405), channel_id=1, source_target_pairs={{0,2},{2,4},{4,6},{6,8},{8,10},{10,12},{12,14},{14,16},{16,18},{18... | collective-permute-start | bytes 30008 | tf_op jit(solution)/shard_map/ppermute | solution.py:42
  222.9 31.0 %copy-start.15 = (f32[5,5,5,5,1,4,1]{6,2,5,0,3,4,1:T(8,128)S(1)}, f32[5,5,5,5,1,4,1]{6,2,5,0,3,4,1:T(8,128)}, u32[]{:S(2)}) copy-start(f32[5,5,5,5,1,4,1]{6,2,5,0,3,4,1:T(8,128)} %copy.407) | copy-start | bytes 30004
  223.6 18.9 %collective-permute-start.15 = (f32[5,5,5,5,1,1,130]{6,5,4,3,2,1,0:T(1,128)S(1)}, f32[5,5,5,5,1,1,130]{6,5,4,3,2,1,0:T(1,128)S(1)}, u32[]{:S(2)}, u32[]{:S(2)}) collective-permute-start(f32[5,5,5,5,1,1,130]{6,5,4,3,2,1,0:T(1,128)S(1)} %copy.410), channel_id=1, source_target_pairs={{1,0},{0,1},{3,2},{2,3},{5,4},{4,5},{7,6},{6,7},{9,8},{8,9},{11,10... | collective-permute-start | bytes 975008 | tf_op jit(solution)/shard_map/ppermute | solution.py:43
  224.5 29.5 %copy-start.12 = (f32[5,5,5,5,1,4,1]{6,2,5,0,3,4,1:T(8,128)S(1)}, f32[5,5,5,5,1,4,1]{6,2,5,0,3,4,1:T(8,128)}, u32[]{:S(2)}) copy-start(f32[5,5,5,5,1,4,1]{6,2,5,0,3,4,1:T(8,128)} %copy.408) | copy-start | bytes 30004
  225.1 28.8 %copy-start.6 = (f32[5,5,5,5,1,4,128]{6,2,5,0,3,4,1:T(8,128)S(1)}, f32[5,5,5,5,1,4,128]{6,2,5,0,3,4,1:T(8,128)}, u32[]{:S(2)}) copy-start(f32[5,5,5,5,1,4,128]{6,2,5,0,3,4,1:T(8,128)} %copy-done.5) | copy-start | bytes 3840004
  225.1 28.7 %collective-permute-start.14 = (f32[5,5,5,5,1,1,130]{6,5,4,3,2,1,0:T(1,128)S(1)}, f32[5,5,5,5,1,1,130]{6,5,4,3,2,1,0:T(1,128)S(1)}, u32[]{:S(2)}, u32[]{:S(2)}) collective-permute-start(f32[5,5,5,5,1,1,130]{6,5,4,3,2,1,0:T(1,128)S(1)} %copy.409), channel_id=1, source_target_pairs={{0,1},{1,0},{2,3},{3,2},{4,5},{5,4},{6,7},{7,6},{8,9},{9,8},{10,11... | collective-permute-start | bytes 975008 | tf_op jit(solution)/shard_map/ppermute | solution.py:42
  313.2 2.8 copy-start.7
  318.4 2.7 copy-start
  325.8 5.5 %collective-permute-start.17 = (f32[5,5,5,5,1,4,1]{3,5,6,4,2,1,0:T(4,128)S(1)}, f32[5,5,5,5,1,4,1]{3,5,6,4,2,1,0:T(4,128)S(1)}, u32[]{:S(2)}, u32[]{:S(2)}) collective-permute-start(f32[5,5,5,5,1,4,1]{3,5,6,4,2,1,0:T(4,128)S(1)} %copy.455), channel_id=1, source_target_pairs={{2,0},{4,2},{6,4},{8,6},{10,8},{12,10},{14,12},{16,14},{18,16},{20... | collective-permute-start | bytes 30008 | tf_op jit(solution)/shard_map/ppermute | solution.py:43
  330.7 9.1 %collective-permute-start.16 = (f32[5,5,5,5,1,4,1]{3,5,6,4,2,1,0:T(4,128)S(1)}, f32[5,5,5,5,1,4,1]{3,5,6,4,2,1,0:T(4,128)S(1)}, u32[]{:S(2)}, u32[]{:S(2)}) collective-permute-start(f32[5,5,5,5,1,4,1]{3,5,6,4,2,1,0:T(4,128)S(1)} %copy.454), channel_id=1, source_target_pairs={{0,2},{2,4},{4,6},{6,8},{8,10},{10,12},{12,14},{14,16},{16,18},{18... | collective-permute-start | bytes 30008 | tf_op jit(solution)/shard_map/ppermute | solution.py:42
  349.6 31.0 %copy-start.16 = (f32[5,5,5,5,1,4,1]{6,1,5,2,0,4,3:T(8,128)S(1)}, f32[5,5,5,5,1,4,1]{6,1,5,2,0,4,3:T(8,128)}, u32[]{:S(2)}) copy-start(f32[5,5,5,5,1,4,1]{6,1,5,2,0,4,3:T(8,128)} %copy.456) | copy-start | bytes 30004
  350.3 18.9 %collective-permute-start.19 = (f32[5,5,5,5,1,1,130]{6,5,4,3,2,1,0:T(1,128)S(1)}, f32[5,5,5,5,1,1,130]{6,5,4,3,2,1,0:T(1,128)S(1)}, u32[]{:S(2)}, u32[]{:S(2)}) collective-permute-start(f32[5,5,5,5,1,1,130]{6,5,4,3,2,1,0:T(1,128)S(1)} %copy.459), channel_id=1, source_target_pairs={{1,0},{0,1},{3,2},{2,3},{5,4},{4,5},{7,6},{6,7},{9,8},{8,9},{11,10... | collective-permute-start | bytes 975008 | tf_op jit(solution)/shard_map/ppermute | solution.py:43
  351.2 29.4 %copy-start.13 = (f32[5,5,5,5,1,4,1]{6,1,5,2,0,4,3:T(8,128)S(1)}, f32[5,5,5,5,1,4,1]{6,1,5,2,0,4,3:T(8,128)}, u32[]{:S(2)}) copy-start(f32[5,5,5,5,1,4,1]{6,1,5,2,0,4,3:T(8,128)} %copy.457) | copy-start | bytes 30004
  351.8 28.8 %copy-start.1 = (f32[5,5,5,5,1,4,128]{6,1,5,2,0,4,3:T(8,128)S(1)}, f32[5,5,5,5,1,4,128]{6,1,5,2,0,4,3:T(8,128)}, u32[]{:S(2)}) copy-start(f32[5,5,5,5,1,4,128]{6,1,5,2,0,4,3:T(8,128)} %copy-done) | copy-start | bytes 3840004
  351.8 28.6 %collective-permute-start.18 = (f32[5,5,5,5,1,1,130]{6,5,4,3,2,1,0:T(1,128)S(1)}, f32[5,5,5,5,1,1,130]{6,5,4,3,2,1,0:T(1,128)S(1)}, u32[]{:S(2)}, u32[]{:S(2)}) collective-permute-start(f32[5,5,5,5,1,1,130]{6,5,4,3,2,1,0:T(1,128)S(1)} %copy.458), channel_id=1, source_target_pairs={{0,1},{1,0},{2,3},{3,2},{4,5},{5,4},{6,7},{7,6},{8,9},{9,8},{10,11... | collective-permute-start | bytes 975008 | tf_op jit(solution)/shard_map/ppermute | solution.py:42
  384.4 9.0 %copy-start.8 = (f32[5,5,5,5,1,6,130]{6,1,5,2,0,4,3:T(8,128)}, f32[5,5,5,5,1,6,130]{6,1,5,2,0,4,3:T(8,128)S(1)}, u32[]{:S(2)}) copy-start(f32[5,5,5,5,1,6,130]{6,1,5,2,0,4,3:T(8,128)S(1)} %maximum_multiply_fusion.2) | copy-start | bytes 5850004
  440.0 1.6 copy-start.2
  442.4 2.7 copy-start.3
  449.7 5.7 %collective-permute-start.21 = (f32[5,5,5,5,1,4,1]{3,5,6,4,2,1,0:T(4,128)S(1)}, f32[5,5,5,5,1,4,1]{3,5,6,4,2,1,0:T(4,128)S(1)}, u32[]{:S(2)}, u32[]{:S(2)}) collective-permute-start(f32[5,5,5,5,1,4,1]{3,5,6,4,2,1,0:T(4,128)S(1)} %copy.502), channel_id=1, source_target_pairs={{2,0},{4,2},{6,4},{8,6},{10,8},{12,10},{14,12},{16,14},{18,16},{20... | collective-permute-start | bytes 30008 | tf_op jit(solution)/shard_map/ppermute | solution.py:43
  454.9 9.1 %collective-permute-start.20 = (f32[5,5,5,5,1,4,1]{3,5,6,4,2,1,0:T(4,128)S(1)}, f32[5,5,5,5,1,4,1]{3,5,6,4,2,1,0:T(4,128)S(1)}, u32[]{:S(2)}, u32[]{:S(2)}) collective-permute-start(f32[5,5,5,5,1,4,1]{3,5,6,4,2,1,0:T(4,128)S(1)} %copy.501), channel_id=1, source_target_pairs={{0,2},{2,4},{4,6},{6,8},{8,10},{10,12},{12,14},{14,16},{16,18},{18... | collective-permute-start | bytes 30008 | tf_op jit(solution)/shard_map/ppermute | solution.py:42
  474.5 18.9 %collective-permute-start.23 = (f32[5,5,5,5,1,1,130]{6,5,4,3,2,1,0:T(1,128)S(1)}, f32[5,5,5,5,1,1,130]{6,5,4,3,2,1,0:T(1,128)S(1)}, u32[]{:S(2)}, u32[]{:S(2)}) collective-permute-start(f32[5,5,5,5,1,1,130]{6,5,4,3,2,1,0:T(1,128)S(1)} %copy.506), channel_id=1, source_target_pairs={{1,0},{0,1},{3,2},{2,3},{5,4},{4,5},{7,6},{6,7},{9,8},{8,9},{11,10... | collective-permute-start | bytes 975008 | tf_op jit(solution)/shard_map/ppermute | solution.py:43
  476.0 28.7 %collective-permute-start.22 = (f32[5,5,5,5,1,1,130]{6,5,4,3,2,1,0:T(1,128)S(1)}, f32[5,5,5,5,1,1,130]{6,5,4,3,2,1,0:T(1,128)S(1)}, u32[]{:S(2)}, u32[]{:S(2)}) collective-permute-start(f32[5,5,5,5,1,1,130]{6,5,4,3,2,1,0:T(1,128)S(1)} %copy.505), channel_id=1, source_target_pairs={{0,1},{1,0},{2,3},{3,2},{4,5},{5,4},{6,7},{7,6},{8,9},{9,8},{10,11... | collective-permute-start | bytes 975008 | tf_op jit(solution)/shard_map/ppermute | solution.py:42
  478.8 26.0 %copy-start.11 = (f32[5,5,5,5,1,4,1]{6,1,5,2,0,4,3:T(8,128)S(1)}, f32[5,5,5,5,1,4,1]{6,1,5,2,0,4,3:T(8,128)}, u32[]{:S(2)}) copy-start(f32[5,5,5,5,1,4,1]{6,1,5,2,0,4,3:T(8,128)} %copy.504) | copy-start | bytes 30004
  478.8 26.0 %copy-start.14 = (f32[5,5,5,5,1,4,1]{6,1,5,2,0,4,3:T(8,128)S(1)}, f32[5,5,5,5,1,4,1]{6,1,5,2,0,4,3:T(8,128)}, u32[]{:S(2)}) copy-start(f32[5,5,5,5,1,4,1]{6,1,5,2,0,4,3:T(8,128)} %copy.503) | copy-start | bytes 30004
  480.2 24.6 %copy-start.4 = (f32[5,5,5,5,1,4,128]{6,1,5,2,0,4,3:T(8,128)S(1)}, f32[5,5,5,5,1,4,128]{6,1,5,2,0,4,3:T(8,128)}, u32[]{:S(2)}) copy-start(f32[5,5,5,5,1,4,128]{6,1,5,2,0,4,3:T(8,128)} %copy-done.3) | copy-start | bytes 3840004
  (6 other events, 6.8 us)
where the time goes:
time: 550 us; the launch traced here: 539 us
  local copies, waits for them, and re-layouts  193 us (35%)
  waiting for transfers between devices  161 us (29%)
  matrix products  76.9 us (14%)
  other arithmetic  74.6 us (14%)
  starting transfers between devices  30.4 us (6%)
    ppermute x7, waiting for transfers between devices, from_behind(): return lax.ppermute(block, axis, route)  62.3 us
    ppermute x8, waiting for transfers between devices, extended_2(): after = lax.ppermute(first, axis, down)  55.3 us
    ppermute x8, waiting for transfers between devices, extended_2(): before = lax.ppermute(last, axis, up)  43.4 us
    slice x12, local copies, waits for them, and re-layouts, extended_2(): last = lax.slice_in_dim(x, length - width, length, axis=dim)  32.7 us
    ppermute x8, local copies, waits for them, and re-layouts, extended_2(): before = lax.ppermute(last, axis, up)  31 us
    ppermute x8, local copies, waits for them, and re-layouts, extended_2(): after = lax.ppermute(first, axis, down)  30.9 us
    scatter-add x4, local copies, waits for them, and re-layouts, apply_core(): result.at[:, :, 4].add(face_term(jacobians[1], 1.0, pitch_hi - in_hi))  23 us
    slice x8, local copies, waits for them, and re-layouts, extended_2(): first = lax.slice_in_dim(x, 0, width, axis=dim)  22.5 us
  transfers between devices with their start and end apart: 24, of which 17 were waited for; matrix products, arithmetic and copies ran while one was open for 18% of the time, Pallas kernels for 0%

commit v1 on v0

v1 whole, which is shorter than its diff:
```python
import functools
import math

import jax
import jax.numpy as jnp
import numpy as np
from jax import lax
from jax.experimental import pallas as pl
from jax.experimental.pallas import tpu as pltpu
from jax.sharding import PartitionSpec as P

SWEEPS = 3
LIFT_HALF = 5.0
INV_DT = 1.5
INV_DTAU = 1.0
DIAG = 12.0
OMEGA = 0.7

LANES = 128
SLICE = 128
SLICES = 20
TRACE = 512
MESH = pl.DeviceIdType.MESH
HIGHEST = lax.Precision.HIGHEST


def gll_derivative():
    nodes = np.array([-1.0, -math.sqrt(3.0 / 7.0), 0.0, math.sqrt(3.0 / 7.0), 1.0])
    legend = (35.0 * nodes**4 - 30.0 * nodes**2 + 3.0) / 8.0
    table = np.zeros((5, 5))
    for left in range(5):
        for right in range(5):
            if left != right:
                table[left, right] = legend[left] / (legend[right] * (nodes[left] - nodes[right]))
    return table


def operator_patterns():
    deriv = gll_derivative()
    planes = np.zeros((13, SLICE, SLICE), np.float32)
    places = [(v, a, p) for v in range(5) for a in range(5) for p in range(5)]
    for q, (v, a, p) in enumerate(places):
        planes[12, q, v] = 1.0
        planes[4, v, q] = 1.0
        planes[3, q, q] = LIFT_HALF * ((a in (0, 4)) + (p in (0, 4)))
        for c, (w, b, r) in enumerate(places):
            planes[0, q, c] = deriv[a, b] * (p == r)
            planes[1, q, c] = deriv[p, r] * (a == b)
            planes[2, q, c] = (a == b) * (p == r)
        for w in range(5):
            for k in range(5):
                low, high, face = 5 * w + k, 32 + 5 * w + k, 64 + 5 * w + k
                if p == 0 and a == k:
                    planes[7, q, low] = -LIFT_HALF
                    planes[8:10, q, low] = -LIFT_HALF * (v == w)
                if p == 4 and a == k:
                    planes[7, q, high] = LIFT_HALF
                    planes[8:10, q, high] = -LIFT_HALF * (v == w)
                if a == 4 and p == k:
                    planes[10, q, face] = LIFT_HALF
                    planes[8, q, face] = -LIFT_HALF * (v == w)
                if a == 0 and p == k:
                    planes[11, q, face] = -LIFT_HALF
                    planes[9, q, face] = -LIFT_HALF * (v == w)
    for w in range(5):
        planes[5, w, 5 * w : 5 * w + 5] = 1.0
        planes[5, w, 32 + 5 * w : 32 + 5 * w + 5] = 1.0
        planes[6, w, 64 + 5 * w : 64 + 5 * w + 5] = 1.0
    return planes


def halves(x):
    high = x.astype(jnp.bfloat16)
    low = (x - high.astype(jnp.float32)).astype(jnp.bfloat16)
    return high, low


def kernel(
    passes,
    state, older, jacobians, offset, planes,
    residual_out, update_out,
    values, resid, trace, turned, ready, facing, pats, spread,
    main_op, ghost_op, face_op, main_x, ghost_x, face_x,
    pack_up, pack_down, from_low, from_high, from_span,
    load_sem, old_sem, trace_sem, pat_sem, out_sem,
    turn_send, turn_recv, face_send, face_recv, halo_send, halo_recv,
):
    row, here, span = lax.axis_index("row"), lax.axis_index("pass"), lax.axis_index("span")
    up, down = lax.rem(here + 1, passes), lax.rem(here + passes - 1, passes)
    tile = TRACE // passes
    deriv = gll_derivative()

    loads = [
        pltpu.make_async_copy(state.at[:, j, 0, :], values.at[0, pl.ds(SLICE * j, 125)], load_sem.at[j])
        for j in range(SLICES)
    ]
    old_loads = [
        pltpu.make_async_copy(older.at[:, j, 0, :], resid.at[j, pl.ds(0, 125)], old_sem.at[j])
        for j in range(SLICES)
    ]
    plane_at = 20 * (1 - row)
    trace_loads = [
        pltpu.make_async_copy(
            state.at[pl.ds(25 * v + plane_at, 5)], trace.at[pl.ds(5 * v, 5)], trace_sem.at[v]
        )
        for v in range(5)
    ]
    pat_load = pltpu.make_async_copy(planes, pats, pat_sem)
    for copy in trace_loads + loads + [pat_load] + old_loads:
        copy.start()

    barrier = pltpu.get_barrier_semaphore()

    def greet(step, carry):
        other = lax.rem(here + step, passes)
        pl.semaphore_signal(barrier, inc=1, device_id=(row, other, span), device_id_type=MESH)
        pl.semaphore_signal(barrier, inc=1, device_id=(1 - row, other, span), device_id_type=MESH)
        return carry

    pl.semaphore_signal(barrier, inc=1, device_id=(row, here, 1 - span), device_id_type=MESH)
    pl.semaphore_signal(barrier, inc=1, device_id=(1 - row, here, span), device_id_type=MESH)
    lax.fori_loop(1, passes, greet, 0)

    for slot in range(2):
        for j in range(SLICES):
            values[slot, pl.ds(SLICE * j + 125, 3), :] = jnp.zeros((3, LANES), jnp.float32)
        values[slot, pl.ds(SLICE * SLICES, 40), :] = jnp.zeros((40, LANES), jnp.float32)
    for j in range(SLICES):
        resid[j, pl.ds(125, 3), :] = jnp.zeros((3, LANES), jnp.float32)
    trace[pl.ds(25, 1)] = jnp.zeros((1, SLICES, 1, LANES), jnp.float32)

    pat_load.wait()
    spread[...] = jnp.zeros_like(spread)
    for d in range(3):
        spread[d, 0:5, 0:5] = jacobians[:, d, :]
    rows = pats[12][:, 0:8]

    def spread_out(d, plane):
        by_row = jnp.dot(rows, spread[d], precision=HIGHEST, preferred_element_type=jnp.float32)
        return jnp.dot(by_row, pats[plane], precision=HIGHEST, preferred_element_type=jnp.float32)

    own = spread_out(0, 4) * pats[0] + spread_out(1, 4) * pats[1] + pats[3]
    along = spread_out(2, 4) * pats[2]
    edges = spread_out(1, 5) * pats[7] + spread_out(0, 6) * pats[10 + row] + pats[8 + row]
    for part, block in enumerate((own, along)):
        for half, piece in enumerate(halves(block)):
            for again in range(2):
                main_op[pl.ds(SLICE * half, SLICE), pl.ds(2 * SLICE * again + SLICE * part, SLICE)] = piece
    for half, piece in enumerate(halves(edges)):
        for again in range(2):
            ghost_op[pl.ds(SLICE * half, SLICE), pl.ds(64 * again, 64)] = piece[:, 0:64]
            face_op[pl.ds(SLICE * half, SLICE), pl.ds(32 * again, 32)] = piece[:, 64:96]

    lane = lax.broadcasted_iota(jnp.int32, (32, LANES), 1)

    def pitch_rows(slot, j, node):
        return values[slot, pl.ds(SLICE * j + node, 32, stride=5), :]

    def halo_copies(slot, t):
        sent = SLICE * (SLICES - 1) * (1 - span)
        return [
            pltpu.make_async_remote_copy(
                src_ref=values.at[slot, pl.ds(pl.multiple_of(sent, SLICE), SLICE)], dst_ref=from_span.at[t],
                send_sem=halo_send.at[0, t], recv_sem=halo_recv.at[0, t],
                device_id=(row, here, 1 - span), device_id_type=MESH),
            pltpu.make_async_remote_copy(
                src_ref=pack_up.at[t], dst_ref=from_low.at[t],
                send_sem=halo_send.at[1, t], recv_sem=halo_recv.at[1, t],
                device_id=(row, up, span), device_id_type=MESH),
            pltpu.make_async_remote_copy(
                src_ref=pack_down.at[t], dst_ref=from_high.at[t],
                send_sem=halo_send.at[2, t], recv_sem=halo_recv.at[2, t],
                device_id=(row, down, span), device_id_type=MESH),
        ]

    def start_halo(slot, t):
        copies = halo_copies(slot, t)
        copies[0].start()
        upward = jnp.zeros((32, LANES), jnp.float32)
        downward = jnp.zeros((32, LANES), jnp.float32)
        for j in range(SLICES):
            upward = jnp.where(lane == j, pltpu.roll(pitch_rows(slot, j, 4), j + 1, 1), upward)
            first = pitch_rows(slot, j, 0)
            downward = jnp.where(lane == j, pltpu.roll(first, j, 1) if j else first, downward)
        pack_up[t] = upward
        pack_down[t] = downward
        copies[1].start()
        copies[2].start()

    def wait_halo(slot, t):
        for copy in halo_copies(slot, t):
            copy.wait()

    def span_ghost(slot, t, elem, low, at, size):
        if low and elem > 0:
            return values[slot, pl.ds(SLICE * (16 + elem - 1) + at, size), :]
        if not low and elem < 3:
            return values[slot, pl.ds(SLICE * (elem + 1) + at, size), :]
        got = from_span[t, pl.ds(at, size), :]
        return jnp.where(span == (1 if low else 0), got, jnp.zeros_like(got))

    def split_main(slot, t, elem):
        cols = pl.ds(LANES * elem, LANES)

        def chunk(c, carry):
            at = pl.multiple_of(16 * c, 16)
            v = [values[slot, pl.ds(pl.multiple_of(SLICE * (4 * s + elem) + at, 16), 16), :] for s in range(5)]
            low = span_ghost(slot, t, elem, True, at, 16)
            high = span_ghost(slot, t, elem, False, at, 16)
            sum04, dif04, sum13, dif13 = v[0] + v[4], v[0] - v[4], v[1] + v[3], v[1] - v[3]
            d = lambda i, j: float(deriv[i, j])
            odd0 = (0.5 * (d(0, 1) + d(0, 3))) * sum13 + d(0, 2) * v[2] + (0.5 * d(0, 4)) * sum04
            even0 = (0.5 * (d(0, 1) - d(0, 3))) * dif13 - (0.5 * d(0, 4)) * dif04
            odd1 = (0.5 * (d(1, 0) + d(1, 4))) * sum04 + d(1, 2) * v[2] + (0.5 * d(1, 3)) * sum13
            even1 = (0.5 * (d(1, 0) - d(1, 4))) * dif04 - (0.5 * d(1, 3)) * dif13
            g = [
                even0 + odd0 - LIFT_HALF * low,
                even1 + odd1,
                d(2, 0) * dif04 + d(2, 1) * dif13,
                even1 - odd1,
                even0 - odd0 + LIFT_HALF * high,
            ]
            for s in range(5):
                for part, block in enumerate((v[s], g[s])):
                    for half, piece in enumerate(halves(block)):
                        place = 2 * SLICE * half + SLICE * part
                        main_x[s, pl.ds(pl.multiple_of(place + at, 16), 16), cols] = piece
            return carry

        lax.fori_loop(0, SLICE // 16, chunk, 0)

    def split_ghosts(slot, t):
        lows, highs = from_low[t], from_high[t]
        for j in range(SLICES):
            cols = pl.ds(LANES * (j % 4), LANES)
            got = pltpu.roll(lows, LANES - j, 1) if j else lows
            low = jnp.where(lane == 0, got, pltpu.roll(pitch_rows(slot, j, 4), 1, 1))
            got = pltpu.roll(highs, LANES - 1 - j, 1)
            high = jnp.where(lane == LANES - 1, got, pltpu.roll(pitch_rows(slot, j, 0), LANES - 1, 1))
            for part, block in enumerate((low, high)):
                for half, piece in enumerate(halves(block)):
                    ghost_x[j // 4, pl.ds(64 * half + 32 * part, 32), cols] = piece

    def apply(slot, t, store):
        for s in range(5):
            image = jnp.dot(main_op[...], main_x[s], preferred_element_type=jnp.float32)
            image = image + jnp.dot(ghost_op[...], ghost_x[s], preferred_element_type=jnp.float32)
            image = image[0:SLICE] + image[SLICE : 2 * SLICE]
            for elem in range(4):
                j = 4 * s + elem
                mine = values[slot, pl.ds(SLICE * j, SLICE), :]
                part = image[:, LANES * elem : LANES * (elem + 1)]
                if s in (0, 4):
                    part = part + LIFT_HALF * (mine - span_ghost(slot, t, elem, s == 0, 0, SLICE))
                store(j, mine, part)

    for copy in trace_loads:
        copy.wait()
    pl.semaphore_wait(barrier, 2 * passes)
    flat = trace.reshape(26 * SLICES, LANES)

    def turn_copy(other):
        return pltpu.make_async_remote_copy(
            src_ref=flat.at[pl.ds(pl.multiple_of(tile * other, tile), tile)], dst_ref=turned.at[here],
            send_sem=turn_send, recv_sem=turn_recv, device_id=(row, other, span), device_id_type=MESH)

    def turn(step, carry):
        turn_copy(lax.rem(here + step, passes)).start()
        return carry

    lax.fori_loop(1, passes, turn, 0)
    turned[here] = flat[pl.ds(pl.multiple_of(tile * here, tile), tile), :]

    for copy in loads:
        copy.wait()
    start_halo(0, 0)
    for elem in (1, 2):
        split_main(0, 0, elem)

    all_turned = pltpu.make_async_remote_copy(
        src_ref=turned.at[pl.ds(0, passes - 1)], dst_ref=turned.at[pl.ds(0, passes - 1)],
        send_sem=turn_send, recv_sem=turn_recv, device_id=(row, up, span), device_id_type=MESH)
    all_turned.wait()
    total = LANES * passes
    shift = lax.rem(lax.rem(offset[0], total) + total, total)
    shift = jnp.where(row == 0, shift, lax.rem(total - shift, total))
    places = shift // LANES
    within = lax.rem(shift, LANES)
    tile_lane = lax.broadcasted_iota(jnp.int32, (tile, LANES), 1)

    def rotate(other, carry):
        near = turned[lax.rem(other - places + passes, passes)]
        far = turned[lax.rem(other - places + 2 * passes - 1, passes)]
        ready[other] = pltpu.roll(jnp.where(tile_lane < LANES - within, near, far), within, 1)
        return carry

    lax.fori_loop(0, passes, rotate, 0)

    def face_copy(other):
        return pltpu.make_async_remote_copy(
            src_ref=ready.at[other], dst_ref=facing.at[pl.ds(pl.multiple_of(tile * here, tile), tile)],
            send_sem=face_send, recv_sem=face_recv, device_id=(1 - row, other, span), device_id_type=MESH)

    def send_face(step, carry):
        face_copy(lax.rem(here + step, passes)).start()
        return carry

    lax.fori_loop(0, passes, send_face, 0)

    wait_halo(0, 0)
    for elem in (0, 3):
        split_main(0, 0, elem)
    split_ghosts(0, 0)
    for copy in old_loads:
        copy.wait()

    def store_residual(j, mine, part):
        resid[j] = INV_DT * (mine - resid[j]) + part

    apply(0, 0, store_residual)

    all_faced = pltpu.make_async_remote_copy(
        src_ref=facing, dst_ref=facing, send_sem=face_send, recv_sem=face_recv,
        device_id=(1 - row, here, span), device_id_type=MESH)
    all_faced.wait()

    for j in range(SLICES):
        block = facing[pl.ds(j, 25, stride=SLICES), :]
        block = jnp.concatenate([block, jnp.zeros((7, LANES), jnp.float32)], axis=0)
        for half, piece in enumerate(halves(block)):
            face_x[j // 4, pl.ds(32 * half, 32), pl.ds(LANES * (j % 4), LANES)] = piece
    outs = [
        pltpu.make_async_copy(resid.at[j, pl.ds(0, 125)], residual_out.at[:, j, 0, :], out_sem.at[0, j])
        for j in range(SLICES)
    ]
    for s in range(5):
        image = jnp.dot(face_op[...], face_x[s], preferred_element_type=jnp.float32)
        image = image[0:SLICE] + image[SLICE : 2 * SLICE]
        for elem in range(4):
            j = 4 * s + elem
            whole = resid[j] + image[:, LANES * elem : LANES * (elem + 1)]
            resid[j] = whole
            values[1, pl.ds(SLICE * j, SLICE), :] = whole * (-1.0 / DIAG)
    for copy in outs:
        copy.start()

    rate = OMEGA / DIAG

    def sweep(t, carry):
        slot = lax.rem(t, 2)
        start_halo(slot, t)
        for elem in (1, 2):
            split_main(slot, t, elem)
        wait_halo(slot, t)
        for elem in (0, 3):
            split_main(slot, t, elem)
        split_ghosts(slot, t)

        def store(j, mine, part):
            image = (INV_DT + INV_DTAU) * mine + part
            values[1 - slot, pl.ds(SLICE * j, SLICE), :] = mine - rate * (resid[j] + image)

        apply(slot, t, store)
        return carry

    lax.fori_loop(1, SWEEPS + 1, sweep, 0)

    last = (SWEEPS + 1) % 2
    final = [
        pltpu.make_async_copy(
            values.at[last, pl.ds(SLICE * j, 125)], update_out.at[:, j, 0, :], out_sem.at[1, j]
        )
        for j in range(SLICES)
    ]
    for copy in final:
        copy.start()
    for copy in outs + final:
        copy.wait()


def per_device(passes, state, old_state, jacobians, offset):
    shape = state.shape
    tile = TRACE // passes
    anywhere = pl.BlockSpec(memory_space=pl.ANY)
    f32, bf16, dma = jnp.float32, jnp.bfloat16, pltpu.SemaphoreType.DMA
    exchanges = SWEEPS + 1
    viewed = (125, SLICES, 1, LANES)
    outs = pl.pallas_call(
        functools.partial(kernel, passes),
        out_shape=[jax.ShapeDtypeStruct(viewed, f32)] * 2,
        in_specs=[anywhere, anywhere, pl.BlockSpec(memory_space=pltpu.VMEM),
                  pl.BlockSpec(memory_space=pltpu.SMEM), anywhere],
        out_specs=[anywhere] * 2,
        scratch_shapes=[
            pltpu.VMEM((2, SLICE * SLICES + 40, LANES), f32),
            pltpu.VMEM((SLICES, SLICE, LANES), f32),
            pltpu.VMEM((26, SLICES, 1, LANES), f32),
            pltpu.VMEM((passes, tile, LANES), f32),
            pltpu.VMEM((passes, tile, LANES), f32),
            pltpu.VMEM((TRACE, LANES), f32),
            pltpu.VMEM((13, SLICE, SLICE), f32),
            pltpu.VMEM((3, 8, LANES), f32),
            pltpu.VMEM((2 * SLICE, 4 * SLICE), bf16),
            pltpu.VMEM((2 * SLICE, 128), bf16),
            pltpu.VMEM((2 * SLICE, 64), bf16),
            pltpu.VMEM((5, 4 * SLICE, 4 * LANES), bf16),
            pltpu.VMEM((5, 128, 4 * LANES), bf16),
            pltpu.VMEM((5, 64, 4 * LANES), bf16),
            pltpu.VMEM((exchanges, 32, LANES), f32),
            pltpu.VMEM((exchanges, 32, LANES), f32),
            pltpu.VMEM((exchanges, 32, LANES), f32),
            pltpu.VMEM((exchanges, 32, LANES), f32),
            pltpu.VMEM((exchanges, SLICE, LANES), f32),
            dma((SLICES,)), dma((SLICES,)), dma((5,)), dma, dma((2, SLICES)),
            dma, dma, dma, dma, dma((3, exchanges)), dma((3, exchanges)),
        ],
        compiler_params=pltpu.CompilerParams(
            collective_id=0, has_side_effects=True, vmem_limit_bytes=48 * 1024 * 1024
        ),
        name="pseudo_step",
    )(
        state.reshape(viewed), old_state.reshape(viewed),
        jnp.transpose(jacobians, (1, 0, 2)), offset, operator_patterns(),
    )
    return tuple(out.reshape(shape) for out in outs)


def solution(mesh):
    placed = P("row", None, None, None, "span", "pass")
    return jax.shard_map(
        functools.partial(per_device, mesh.shape["pass"]),
        mesh=mesh,
        in_specs=(placed, placed, P(), P()),
        out_specs=(placed, placed),
        check_vma=False,
    )
```

time: 550 us -> 66.6 us (0.12)
  the two profiles are of different devices: /device:TPU:4 before, /device:TPU:2 now
where the time goes in v1:
time: 66.6 us; the launch traced here: 66.3 us
  Pallas kernels  58.5 us (88%)
  local copies, waits for them, and re-layouts  6.55 us (10%)
  between operations  1.3 us (2%)
    pallas_call x1, Pallas kernels, per_device(): pl.pallas_call(functools.partial(kernel, passes), out_shape=[jax.ShapeDty...  58.5 us
    unnamed x10, local copies, waits for them, and re-layouts  6.55 us

profile of v1, /device:TPU:2, one launch (start us, length us, event | category | flops | bytes accessed | tf_op | source)
XLA Modules:
  0.0 66.3 jit_solution(4620699091100739916)
XLA Ops:
  1.3 0.0 copy-start
  1.3 1.3 %copy-done = f32[1,5,125,1,4,128]{5,4,3,2,1,0:T(4,128)S(1)} copy-done((f32[1,5,125,1,4,128]{5,4,3,2,1,0:T(4,128)S(1)}, f32[1,5,125,1,4,128]{5,4,3,2,1,0:T(4,128)}, u32[]{:S(2)}) %copy-start) | copy-done | bytes 1280024
  2.6 0.0 copy-start.1
  2.6 1.3 %copy-done.1 = f32[1,5,125,1,4,128]{5,4,3,2,1,0:T(4,128)S(1)} copy-done((f32[1,5,125,1,4,128]{5,4,3,2,1,0:T(4,128)S(1)}, f32[1,5,125,1,4,128]{5,4,3,2,1,0:T(4,128)}, u32[]{:S(2)}) %copy-start.1) | copy-done | bytes 1280024
  3.9 0.0 copy-start.2
  3.9 1.2 %copy-done.2 = f32[13,128,128]{2,1,0:T(8,128)S(1)} copy-done((f32[13,128,128]{2,1,0:T(8,128)S(1)}, f32[13,128,128]{2,1,0:T(8,128)}, u32[]{:S(2)}) %copy-start.2) | copy-done | bytes 851992
  5.0 0.0 copy-start.3
  5.0 0.7 %copy-done.3 = f32[3,5,5]{2,0,1:T(4,128)S(1)} copy-done((f32[3,5,5]{2,0,1:T(4,128)S(1)}, f32[3,5,5]{2,0,1:T(4,128)}, u32[]{:S(2)}) %copy-start.3) | copy-done | bytes 324
  5.7 58.5 %pseudo_step.1 = (f32[125,20,1,128]{3,2,1,0:T(1,128)S(1)}, f32[125,20,1,128]{3,2,1,0:T(1,128)S(1)}) custom-call(f32[125,20,1,128]{3,2,1,0:T(1,128)S(1)} %bitcast.11, f32[125,20,1,128]{3,2,1,0:T(1,128)S(1)} %bitcast.12, f32[5,3,5]{2,1,0:T(4,128)S(1)} %bitcast.13, s32[1]{0:T(128)S(6)} %copy.11.offset, f32[13,128,128]{2,1,0:T(8,128)S(1)} %copy-done.2), custom_call_target="tpu_custom_call" | custom-call | tf_op jit(solution)/shard_map/pseudo_step/pallas_call | solution.py:388
  64.2 1.0 %copy.12 = f32[1,5,125,1,4,128]{5,4,3,2,1,0:T(4,128)} copy(f32[1,5,125,1,4,128]{5,4,3,2,1,0:T(4,128)S(1)} %bitcast.10) | data formatting | bytes 2560000
  65.3 1.0 %copy.13 = f32[1,5,125,1,4,128]{5,4,3,2,1,0:T(4,128)} copy(f32[1,5,125,1,4,128]{5,4,3,2,1,0:T(4,128)S(1)} %bitcast.9) | data formatting | bytes 2560000
Async XLA Ops:
  1.3 1.3 %copy-start = (f32[1,5,125,1,4,128]{5,4,3,2,1,0:T(4,128)S(1)}, f32[1,5,125,1,4,128]{5,4,3,2,1,0:T(4,128)}, u32[]{:S(2)}) copy-start(f32[1,5,125,1,4,128]{5,4,3,2,1,0:T(4,128)} %param.5) | copy-start | bytes 3840004
  2.6 1.3 %copy-start.1 = (f32[1,5,125,1,4,128]{5,4,3,2,1,0:T(4,128)S(1)}, f32[1,5,125,1,4,128]{5,4,3,2,1,0:T(4,128)}, u32[]{:S(2)}) copy-start(f32[1,5,125,1,4,128]{5,4,3,2,1,0:T(4,128)} %param.6) | copy-start | bytes 3840004
  3.9 1.2 %copy-start.2 = (f32[13,128,128]{2,1,0:T(8,128)S(1)}, f32[13,128,128]{2,1,0:T(8,128)}, u32[]{:S(2)}) copy-start(f32[13,128,128]{2,1,0:T(8,128)} %constant.2.clone.planes) | copy-start | bytes 2555908
  5.0 0.7 %copy-start.3 = (f32[3,5,5]{2,0,1:T(4,128)S(1)}, f32[3,5,5]{2,0,1:T(4,128)}, u32[]{:S(2)}) copy-start(f32[3,5,5]{2,0,1:T(4,128)} %param.7) | copy-start | bytes 904

commit v2 on v1

--- a/solution.py
+++ b/solution.py
@@ -80,15 +80,35 @@
     state, older, jacobians, offset, planes,
     residual_out, update_out,
     values, resid, trace, turned, ready, facing, pats, spread,
-    main_op, ghost_op, face_op, main_x, ghost_x, face_x,
+    jacs, main_op, ghost_op, face_op, main_x, ghost_x, face_x,
     pack_up, pack_down, from_low, from_high, from_span,
-    load_sem, old_sem, trace_sem, pat_sem, out_sem,
+    load_sem, old_sem, trace_sem, pat_sem, jac_sem, out_sem,
     turn_send, turn_recv, face_send, face_recv, halo_send, halo_recv,
 ):
     row, here, span = lax.axis_index("row"), lax.axis_index("pass"), lax.axis_index("span")
     up, down = lax.rem(here + 1, passes), lax.rem(here + passes - 1, passes)
     tile = TRACE // passes
     deriv = gll_derivative()
+
+    def peer(step):
+        turn_z, turn_y, turn_core = step // 8, lax.rem(step // 2, 4), lax.rem(step + 1, 2)
+        along_z = 4 + (1 - 2 * lax.rem(turn_z, 2)) * ((turn_z + 1) // 2)
+        along_y = 2 + (1 - 2 * lax.rem(turn_y, 2)) * ((turn_y + 1) // 2)
+        y = lax.rem(here // 16 + along_y, 4)
+        z = lax.rem(here // 2 + along_z, 8)
+        return 16 * y + 2 * z + lax.rem(here + turn_core, 2)
+
+    barrier = pltpu.get_barrier_semaphore()
+
+    def greet(step, carry):
+        other = peer(step)
+        pl.semaphore_signal(barrier, inc=1, device_id=(1 - row, other, span), device_id_type=MESH)
+        pl.semaphore_signal(barrier, inc=1, device_id=(row, other, span), device_id_type=MESH)
+        return carry
+
+    lax.fori_loop(0, passes - 1, greet, 0)
+    pl.semaphore_signal(barrier, inc=1, device_id=(1 - row, here, span), device_id_type=MESH)
+    pl.semaphore_signal(barrier, inc=1, device_id=(row, here, 1 - span), device_id_type=MESH)
 
     loads = [
         pltpu.make_async_copy(state.at[:, j, 0, :], values.at[0, pl.ds(SLICE * j, 125)], load_sem.at[j])
@@ -106,50 +126,9 @@
         for v in range(5)
     ]
     pat_load = pltpu.make_async_copy(planes, pats, pat_sem)
-    for copy in trace_loads + loads + [pat_load] + old_loads:
+    jac_load = pltpu.make_async_copy(jacobians, jacs, jac_sem)
+    for copy in trace_loads + loads + [pat_load, jac_load] + old_loads:
         copy.start()
-
-    barrier = pltpu.get_barrier_semaphore()
-
-    def greet(step, carry):
-        other = lax.rem(here + step, passes)
-        pl.semaphore_signal(barrier, inc=1, device_id=(row, other, span), device_id_type=MESH)
-        pl.semaphore_signal(barrier, inc=1, device_id=(1 - row, other, span), device_id_type=MESH)
-        return carry
-
-    pl.semaphore_signal(barrier, inc=1, device_id=(row, here, 1 - span), device_id_type=MESH)
-    pl.semaphore_signal(barrier, inc=1, device_id=(1 - row, here, span), device_id_type=MESH)
-    lax.fori_loop(1, passes, greet, 0)
-
-    for slot in range(2):
-        for j in range(SLICES):
-            values[slot, pl.ds(SLICE * j + 125, 3), :] = jnp.zeros((3, LANES), jnp.float32)
-        values[slot, pl.ds(SLICE * SLICES, 40), :] = jnp.zeros((40, LANES), jnp.float32)
-    for j in range(SLICES):
-        resid[j, pl.ds(125, 3), :] = jnp.zeros((3, LANES), jnp.float32)
-    trace[pl.ds(25, 1)] = jnp.zeros((1, SLICES, 1, LANES), jnp.float32)
-
-    pat_load.wait()
-    spread[...] = jnp.zeros_like(spread)
-    for d in range(3):
-        spread[d, 0:5, 0:5] = jacobians[:, d, :]
-    rows = pats[12][:, 0:8]
-
-    def spread_out(d, plane):
-        by_row = jnp.dot(rows, spread[d], precision=HIGHEST, preferred_element_type=jnp.float32)
-        return jnp.dot(by_row, pats[plane], precision=HIGHEST, preferred_element_type=jnp.float32)
-
-    own = spread_out(0, 4) * pats[0] + spread_out(1, 4) * pats[1] + pats[3]
-    along = spread_out(2, 4) * pats[2]
-    edges = spread_out(1, 5) * pats[7] + spread_out(0, 6) * pats[10 + row] + pats[8 + row]
-    for part, block in enumerate((own, along)):
-        for half, piece in enumerate(halves(block)):
-            for again in range(2):
-                main_op[pl.ds(SLICE * half, SLICE), pl.ds(2 * SLICE * again + SLICE * part, SLICE)] = piece
-    for half, piece in enumerate(halves(edges)):
-        for again in range(2):
-            ghost_op[pl.ds(SLICE * half, SLICE), pl.ds(64 * again, 64)] = piece[:, 0:64]
-            face_op[pl.ds(SLICE * half, SLICE), pl.ds(32 * again, 32)] = piece[:, 64:96]
 
     lane = lax.broadcasted_iota(jnp.int32, (32, LANES), 1)
 
@@ -254,6 +233,7 @@
                     part = part + LIFT_HALF * (mine - span_ghost(slot, t, elem, s == 0, 0, SLICE))
                 store(j, mine, part)
 
+    trace[pl.ds(25, 1)] = jnp.zeros((1, SLICES, 1, LANES), jnp.float32)
     for copy in trace_loads:
         copy.wait()
     pl.semaphore_wait(barrier, 2 * passes)
@@ -265,11 +245,41 @@
             send_sem=turn_send, recv_sem=turn_recv, device_id=(row, other, span), device_id_type=MESH)
 
     def turn(step, carry):
-        turn_copy(lax.rem(here + step, passes)).start()
+        turn_copy(peer(step)).start()
         return carry
 
-    lax.fori_loop(1, passes, turn, 0)
+    lax.fori_loop(0, passes - 1, turn, 0)
     turned[here] = flat[pl.ds(pl.multiple_of(tile * here, tile), tile), :]
+
+    for slot in range(2):
+        for j in range(SLICES):
+            values[slot, pl.ds(SLICE * j + 125, 3), :] = jnp.zeros((3, LANES), jnp.float32)
+        values[slot, pl.ds(SLICE * SLICES, 40), :] = jnp.zeros((40, LANES), jnp.float32)
+    for j in range(SLICES):
+        resid[j, pl.ds(125, 3), :] = jnp.zeros((3, LANES), jnp.float32)
+
+    pat_load.wait()
+    jac_load.wait()
+    spread[...] = jnp.zeros_like(spread)
+    for d in range(3):
+        spread[d, 0:5, 0:5] = jacs[:, d, :]
+    rows = pats[12][:, 0:8]
+
+    def spread_out(d, plane):
+        by_row = jnp.dot(rows, spread[d], precision=HIGHEST, preferred_element_type=jnp.float32)
+        return jnp.dot(by_row, pats[plane], precision=HIGHEST, preferred_element_type=jnp.float32)
+
+    own = spread_out(0, 4) * pats[0] + spread_out(1, 4) * pats[1] + pats[3]
+    along = spread_out(2, 4) * pats[2]
+    edges = spread_out(1, 5) * pats[7] + spread_out(0, 6) * pats[10 + row] + pats[8 + row]
+    for part, block in enumerate((own, along)):
+        for half, piece in enumerate(halves(block)):
+            for again in range(2):
+                main_op[pl.ds(SLICE * half, SLICE), pl.ds(2 * SLICE * again + SLICE * part, SLICE)] = piece
+    for half, piece in enumerate(halves(edges)):
+        for again in range(2):
+            ghost_op[pl.ds(SLICE * half, SLICE), pl.ds(64 * again, 64)] = piece[:, 0:64]
+            face_op[pl.ds(SLICE * half, SLICE), pl.ds(32 * again, 32)] = piece[:, 64:96]
 
     for copy in loads:
         copy.wait()
@@ -288,24 +298,18 @@
     within = lax.rem(shift, LANES)
     tile_lane = lax.broadcasted_iota(jnp.int32, (tile, LANES), 1)
 
-    def rotate(other, carry):
+    def rotate(step, carry):
+        other = peer(step)
         near = turned[lax.rem(other - places + passes, passes)]
         far = turned[lax.rem(other - places + 2 * passes - 1, passes)]
         ready[other] = pltpu.roll(jnp.where(tile_lane < LANES - within, near, far), within, 1)
+        pltpu.make_async_remote_copy(
+            src_ref=ready.at[other], dst_ref=facing.at[pl.ds(pl.multiple_of(tile * here, tile), tile)],
+            send_sem=face_send, recv_sem=face_recv, device_id=(1 - row, other, span), device_id_type=MESH,
+        ).start()
         return carry
 
-    lax.fori_loop(0, passes, rotate, 0)
-
-    def face_copy(other):
-        return pltpu.make_async_remote_copy(
-            src_ref=ready.at[other], dst_ref=facing.at[pl.ds(pl.multiple_of(tile * here, tile), tile)],
-            send_sem=face_send, recv_sem=face_recv, device_id=(1 - row, other, span), device_id_type=MESH)
-
-    def send_face(step, carry):
-        face_copy(lax.rem(here + step, passes)).start()
-        return carry
-
-    lax.fori_loop(0, passes, send_face, 0)
+    lax.fori_loop(0, passes, rotate, 0, unroll=4)
 
     wait_halo(0, 0)
     for elem in (0, 3):
@@ -382,14 +386,16 @@
     shape = state.shape
     tile = TRACE // passes
     anywhere = pl.BlockSpec(memory_space=pl.ANY)
+    in_hbm = pl.BlockSpec(memory_space=pltpu.HBM)
     f32, bf16, dma = jnp.float32, jnp.bfloat16, pltpu.SemaphoreType.DMA
     exchanges = SWEEPS + 1
     viewed = (125, SLICES, 1, LANES)
+    pinned = lambda x: pltpu.with_memory_space_constraint(x, pltpu.HBM)
     outs = pl.pallas_call(
         functools.partial(kernel, passes),
         out_shape=[jax.ShapeDtypeStruct(viewed, f32)] * 2,
-        in_specs=[anywhere, anywhere, pl.BlockSpec(memory_space=pltpu.VMEM),
-                  pl.BlockSpec(memory_space=pltpu.SMEM), anywhere],
+        in_specs=[in_hbm, in_hbm, in_hbm,
+                  pl.BlockSpec(memory_space=pltpu.SMEM), in_hbm],
         out_specs=[anywhere] * 2,
         scratch_shapes=[
             pltpu.VMEM((2, SLICE * SLICES + 40, LANES), f32),
@@ -400,6 +406,7 @@
             pltpu.VMEM((TRACE, LANES), f32),
             pltpu.VMEM((13, SLICE, SLICE), f32),
             pltpu.VMEM((3, 8, LANES), f32),
+            pltpu.VMEM((5, 3, 5), f32),
             pltpu.VMEM((2 * SLICE, 4 * SLICE), bf16),
             pltpu.VMEM((2 * SLICE, 128), bf16),
             pltpu.VMEM((2 * SLICE, 64), bf16),
@@ -411,7 +418,7 @@
             pltpu.VMEM((exchanges, 32, LANES), f32),
             pltpu.VMEM((exchanges, 32, LANES), f32),
             pltpu.VMEM((exchanges, SLICE, LANES), f32),
-            dma((SLICES,)), dma((SLICES,)), dma((5,)), dma, dma((2, SLICES)),
+            dma((SLICES,)), dma((SLICES,)), dma((5,)), dma, dma, dma((2, SLICES)),
             dma, dma, dma, dma, dma((3, exchanges)), dma((3, exchanges)),
         ],
         compiler_params=pltpu.CompilerParams(
@@ -419,8 +426,8 @@
         ),
         name="pseudo_step",
     )(
-        state.reshape(viewed), old_state.reshape(viewed),
-        jnp.transpose(jacobians, (1, 0, 2)), offset, operator_patterns(),
+        pinned(state.reshape(viewed)), pinned(old_state.reshape(viewed)),
+        pinned(jnp.transpose(jacobians, (1, 0, 2))), offset, pinned(jnp.asarray(operator_patterns())),
     )
     return tuple(out.reshape(shape) for out in outs)
 

time: 66.6 us -> 57.2 us (0.86)
  Pallas kernels: 58.5 us -> 53.7 us
  local copies, waits for them, and re-layouts: 6.55 us -> 2.09 us
    pallas_call x1, Pallas kernels: 58.5 us -> 53.7 us  [per_device(): pl.pallas_call(functools.partial(kernel, passes), out_shape=[jax.ShapeDty...]
    unnamed x10 -> x2, local copies, waits for them, and re-layouts: 6.55 us -> 2.09 us
where the time goes in v2:
time: 57.2 us; the launch traced here: 57.1 us
  Pallas kernels  53.7 us (94%)
  local copies, waits for them, and re-layouts  2.09 us (4%)
  between operations  1.29 us (2%)
    pallas_call x1, Pallas kernels, per_device(): pl.pallas_call(functools.partial(kernel, passes), out_shape=[jax.ShapeDty...  53.7 us
    unnamed x2, local copies, waits for them, and re-layouts  2.09 us

profile of v2, /device:TPU:2, one launch (start us, length us, event | category | flops | bytes accessed | tf_op | source)
XLA Modules:
  0.0 57.1 jit_solution(17291050348281783822)
XLA Ops:
  1.3 53.7 %pseudo_step.1 = (f32[125,20,1,128]{3,2,1,0:T(1,128)S(1)}, f32[125,20,1,128]{3,2,1,0:T(1,128)S(1)}) custom-call(f32[125,20,1,128]{3,2,1,0:T(1,128)} %bitcast.11, f32[125,20,1,128]{3,2,1,0:T(1,128)} %bitcast.12, f32[5,3,5]{2,1,0:T(4,128)} %bitcast.13, s32[1]{0:T(128)S(6)} %copy.11.offset, f32[13,128,128]{2,1,0:T(8,128)} %constant.2.clone.planes), custom_call_target="tpu_custom_call" | custom-call | tf_op jit(solution)/shard_map/pseudo_step/pallas_call | solution.py:394
  55.0 1.0 %copy.12 = f32[1,5,125,1,4,128]{5,4,3,2,1,0:T(4,128)} copy(f32[1,5,125,1,4,128]{5,4,3,2,1,0:T(4,128)S(1)} %bitcast.10) | data formatting | bytes 2560000
  56.1 1.0 %copy.13 = f32[1,5,125,1,4,128]{5,4,3,2,1,0:T(4,128)} copy(f32[1,5,125,1,4,128]{5,4,3,2,1,0:T(4,128)S(1)} %bitcast.9) | data formatting | bytes 2560000

commit v3 on v2

--- a/solution.py
+++ b/solution.py
@@ -78,13 +78,14 @@
 def kernel(
     passes,
     state, older, jacobians, offset, planes,
-    residual_out, update_out,
-    values, resid, trace, turned, ready, facing, pats, spread,
-    jacs, main_op, ghost_op, face_op, main_x, ghost_x, face_x,
+    resid_rows, update_rows,
+    resid, even, odd, trace, turned, ready, facing, pats, spread, jacs, edge_rows,
+    main_op, face_op, span_op, pitch_op, main_x, face_x,
     pack_up, pack_down, from_low, from_high, from_span,
-    load_sem, old_sem, trace_sem, pat_sem, jac_sem, out_sem,
+    load_sem, old_sem, trace_sem, pat_sem, jac_sem,
     turn_send, turn_recv, face_send, face_recv, halo_send, halo_recv,
 ):
+    values = (even, odd)
     row, here, span = lax.axis_index("row"), lax.axis_index("pass"), lax.axis_index("span")
     up, down = lax.rem(here + 1, passes), lax.rem(here + passes - 1, passes)
     tile = TRACE // passes
@@ -111,11 +112,11 @@
     pl.semaphore_signal(barrier, inc=1, device_id=(row, here, 1 - span), device_id_type=MESH)
 
     loads = [
-        pltpu.make_async_copy(state.at[:, j, 0, :], values.at[0, pl.ds(SLICE * j, 125)], load_sem.at[j])
+        pltpu.make_async_copy(state.at[:, j, 0, :], even.at[pl.ds(SLICE * j, 125)], load_sem.at[j])
         for j in range(SLICES)
     ]
     old_loads = [
-        pltpu.make_async_copy(older.at[:, j, 0, :], resid.at[j, pl.ds(0, 125)], old_sem.at[j])
+        pltpu.make_async_copy(older.at[:, j, 0, :], resid.at[pl.ds(SLICE * j, 125)], old_sem.at[j])
         for j in range(SLICES)
     ]
     plane_at = 20 * (1 - row)
@@ -131,17 +132,20 @@
         copy.start()
 
     lane = lax.broadcasted_iota(jnp.int32, (32, LANES), 1)
-
-    def pitch_rows(slot, j, node):
-        return values[slot, pl.ds(SLICE * j + node, 32, stride=5), :]
-
-    def halo_copies(slot, t):
-        sent = SLICE * (SLICES - 1) * (1 - span)
+    sent = (SLICES - 1) * (1 - span)
+    sent_rows = pl.ds(pl.multiple_of(SLICE * sent, SLICE), SLICE)
+
+    def pitch_rows(field, j, node):
+        return field[pl.ds(SLICE * j + node, 32, stride=5), :]
+
+    def span_copy(field, t):
+        return pltpu.make_async_remote_copy(
+            src_ref=field.at[sent_rows], dst_ref=from_span.at[t],
+            send_sem=halo_send.at[0, t], recv_sem=halo_recv.at[0, t],
+            device_id=(row, here, 1 - span), device_id_type=MESH)
+
+    def pitch_copies(t):
         return [
-            pltpu.make_async_remote_copy(
-                src_ref=values.at[slot, pl.ds(pl.multiple_of(sent, SLICE), SLICE)], dst_ref=from_span.at[t],
-                send_sem=halo_send.at[0, t], recv_sem=halo_recv.at[0, t],
-                device_id=(row, here, 1 - span), device_id_type=MESH),
             pltpu.make_async_remote_copy(
                 src_ref=pack_up.at[t], dst_ref=from_low.at[t],
                 send_sem=halo_send.at[1, t], recv_sem=halo_recv.at[1, t],
@@ -152,40 +156,22 @@
                 device_id=(row, down, span), device_id_type=MESH),
         ]
 
-    def start_halo(slot, t):
-        copies = halo_copies(slot, t)
-        copies[0].start()
+    def packed(field):
         upward = jnp.zeros((32, LANES), jnp.float32)
         downward = jnp.zeros((32, LANES), jnp.float32)
         for j in range(SLICES):
-            upward = jnp.where(lane == j, pltpu.roll(pitch_rows(slot, j, 4), j + 1, 1), upward)
-            first = pitch_rows(slot, j, 0)
+            upward = jnp.where(lane == j, pltpu.roll(pitch_rows(field, j, 4), j + 1, 1), upward)
+            first = pitch_rows(field, j, 0)
             downward = jnp.where(lane == j, pltpu.roll(first, j, 1) if j else first, downward)
-        pack_up[t] = upward
-        pack_down[t] = downward
-        copies[1].start()
-        copies[2].start()
-
-    def wait_halo(slot, t):
-        for copy in halo_copies(slot, t):
-            copy.wait()
-
-    def span_ghost(slot, t, elem, low, at, size):
-        if low and elem > 0:
-            return values[slot, pl.ds(SLICE * (16 + elem - 1) + at, size), :]
-        if not low and elem < 3:
-            return values[slot, pl.ds(SLICE * (elem + 1) + at, size), :]
-        got = from_span[t, pl.ds(at, size), :]
-        return jnp.where(span == (1 if low else 0), got, jnp.zeros_like(got))
-
-    def split_main(slot, t, elem):
+        return upward, downward
+
+    def split_main(field, elem):
         cols = pl.ds(LANES * elem, LANES)
 
         def chunk(c, carry):
             at = pl.multiple_of(16 * c, 16)
-            v = [values[slot, pl.ds(pl.multiple_of(SLICE * (4 * s + elem) + at, 16), 16), :] for s in range(5)]
-            low = span_ghost(slot, t, elem, True, at, 16)
-            high = span_ghost(slot, t, elem, False, at, 16)
+            load = lambda j: field[pl.ds(pl.multiple_of(SLICE * j + at, 16), 16), :]
+            v = [load(4 * s + elem) for s in range(5)]
             sum04, dif04, sum13, dif13 = v[0] + v[4], v[0] - v[4], v[1] + v[3], v[1] - v[3]
             d = lambda i, j: float(deriv[i, j])
             odd0 = (0.5 * (d(0, 1) + d(0, 3))) * sum13 + d(0, 2) * v[2] + (0.5 * d(0, 4)) * sum04
@@ -193,12 +179,16 @@
             odd1 = (0.5 * (d(1, 0) + d(1, 4))) * sum04 + d(1, 2) * v[2] + (0.5 * d(1, 3)) * sum13
             even1 = (0.5 * (d(1, 0) - d(1, 4))) * dif04 - (0.5 * d(1, 3)) * dif13
             g = [
-                even0 + odd0 - LIFT_HALF * low,
+                even0 + odd0,
                 even1 + odd1,
                 d(2, 0) * dif04 + d(2, 1) * dif13,
                 even1 - odd1,
-                even0 - odd0 + LIFT_HALF * high,
+                even0 - odd0,
             ]
+            if elem > 0:
+                g[0] = g[0] - LIFT_HALF * load(16 + elem - 1)
+            if elem < 3:
+                g[4] = g[4] + LIFT_HALF * load(elem + 1)
             for s in range(5):
                 for part, block in enumerate((v[s], g[s])):
                     for half, piece in enumerate(halves(block)):
@@ -208,30 +198,68 @@
 
         lax.fori_loop(0, SLICE // 16, chunk, 0)
 
-    def split_ghosts(slot, t):
-        lows, highs = from_low[t], from_high[t]
+    def split_ghosts(field):
         for j in range(SLICES):
             cols = pl.ds(LANES * (j % 4), LANES)
-            got = pltpu.roll(lows, LANES - j, 1) if j else lows
-            low = jnp.where(lane == 0, got, pltpu.roll(pitch_rows(slot, j, 4), 1, 1))
-            got = pltpu.roll(highs, LANES - 1 - j, 1)
-            high = jnp.where(lane == LANES - 1, got, pltpu.roll(pitch_rows(slot, j, 0), LANES - 1, 1))
+            low = jnp.where(lane == 0, 0.0, pltpu.roll(pitch_rows(field, j, 4), 1, 1))
+            high = jnp.where(lane == LANES - 1, 0.0, pltpu.roll(pitch_rows(field, j, 0), LANES - 1, 1))
             for part, block in enumerate((low, high)):
                 for half, piece in enumerate(halves(block)):
-                    ghost_x[j // 4, pl.ds(64 * half + 32 * part, 32), cols] = piece
-
-    def apply(slot, t, store):
+                    main_x[j // 4, pl.ds(4 * SLICE + 64 * half + 32 * part, 32), cols] = piece
+
+    def apply(field, store):
+        for elem in range(4):
+            split_main(field, elem)
+        split_ghosts(field)
         for s in range(5):
             image = jnp.dot(main_op[...], main_x[s], preferred_element_type=jnp.float32)
-            image = image + jnp.dot(ghost_op[...], ghost_x[s], preferred_element_type=jnp.float32)
             image = image[0:SLICE] + image[SLICE : 2 * SLICE]
             for elem in range(4):
                 j = 4 * s + elem
-                mine = values[slot, pl.ds(SLICE * j, SLICE), :]
+                mine = field[pl.ds(SLICE * j, SLICE), :]
                 part = image[:, LANES * elem : LANES * (elem + 1)]
                 if s in (0, 4):
-                    part = part + LIFT_HALF * (mine - span_ghost(slot, t, elem, s == 0, 0, SLICE))
+                    jump = mine
+                    if s == 0 and elem > 0:
+                        jump = mine - field[pl.ds(SLICE * (16 + elem - 1), SLICE), :]
+                    if s == 4 and elem < 3:
+                        jump = mine - field[pl.ds(SLICE * (elem + 1), SLICE), :]
+                    part = part + LIFT_HALF * jump
                 store(j, mine, part)
+
+    def correct(field, t, factor, send_on):
+        if send_on:
+            upward, downward = packed(field)
+        for copy in pitch_copies(t):
+            copy.wait()
+        pieces = [piece for got in (from_low[t], from_high[t]) for piece in halves(got)]
+        edge = jnp.dot(pitch_op[...], jnp.concatenate(pieces, 0), preferred_element_type=jnp.float32)
+        low = factor * (edge[0:32] + edge[32:64])
+        high = factor * (edge[64:96] + edge[96:128])
+        span_copy(field, t).wait()
+        share = jnp.dot(span_op[...], jnp.concatenate(halves(from_span[t]), 0), preferred_element_type=jnp.float32)
+        field[sent_rows, :] = field[sent_rows, :] + factor * (share[0:SLICE] + share[SLICE : 2 * SLICE])
+
+        def columns(j):
+            at_low = pl.ds(SLICE * j, 25, stride=5)
+            at_high = pl.ds(SLICE * j + 4, 25, stride=5)
+            came = pltpu.roll(low, lax.rem(LANES - j, LANES), 1)
+            field[at_low, :] = field[at_low, :] + jnp.where(lane == 0, came, 0.0)[0:25]
+            came = pltpu.roll(high, LANES - 1 - j, 1)
+            field[at_high, :] = field[at_high, :] + jnp.where(lane == LANES - 1, came, 0.0)[0:25]
+
+        columns(sent)
+        if send_on:
+            span_copy(field, t + 1).start()
+            last = pltpu.roll(pitch_rows(field, sent, 4), sent + 1, 1)
+            first = pltpu.roll(pitch_rows(field, sent, 0), sent, 1)
+            pack_up[t + 1] = jnp.where(lane == sent, last, upward + high)
+            pack_down[t + 1] = jnp.where(lane == sent, first, downward + low)
+            for copy in pitch_copies(t + 1):
+                copy.start()
+        columns(SLICES - 1 - sent)
+        for j in range(1, SLICES - 1):
+            columns(j)
 
     trace[pl.ds(25, 1)] = jnp.zeros((1, SLICES, 1, LANES), jnp.float32)
     for copy in trace_loads:
@@ -251,12 +279,11 @@
     lax.fori_loop(0, passes - 1, turn, 0)
     turned[here] = flat[pl.ds(pl.multiple_of(tile * here, tile), tile), :]
 
-    for slot in range(2):
+    for field in (even, resid):
         for j in range(SLICES):
-            values[slot, pl.ds(SLICE * j + 125, 3), :] = jnp.zeros((3, LANES), jnp.float32)
-        values[slot, pl.ds(SLICE * SLICES, 40), :] = jnp.zeros((40, LANES), jnp.float32)
-    for j in range(SLICES):
-        resid[j, pl.ds(125, 3), :] = jnp.zeros((3, LANES), jnp.float32)
+            field[pl.ds(SLICE * j + 125, 3), :] = jnp.zeros((3, LANES), jnp.float32)
+    for field in (even, odd):
+        field[pl.ds(SLICE * SLICES, 40), :] = jnp.zeros((40, LANES), jnp.float32)
 
     pat_load.wait()
     jac_load.wait()
@@ -272,20 +299,36 @@
     own = spread_out(0, 4) * pats[0] + spread_out(1, 4) * pats[1] + pats[3]
     along = spread_out(2, 4) * pats[2]
     edges = spread_out(1, 5) * pats[7] + spread_out(0, 6) * pats[10 + row] + pats[8 + row]
-    for part, block in enumerate((own, along)):
-        for half, piece in enumerate(halves(block)):
+    for half in range(2):
+        op_rows = pl.ds(SLICE * half, SLICE)
+        for part, block in enumerate((own, along)):
+            piece = halves(block)[half]
             for again in range(2):
-                main_op[pl.ds(SLICE * half, SLICE), pl.ds(2 * SLICE * again + SLICE * part, SLICE)] = piece
-    for half, piece in enumerate(halves(edges)):
+                main_op[op_rows, pl.ds(2 * SLICE * again + SLICE * part, SLICE)] = piece
+        piece = halves(edges)[half]
         for again in range(2):
-            ghost_op[pl.ds(SLICE * half, SLICE), pl.ds(64 * again, 64)] = piece[:, 0:64]
-            face_op[pl.ds(SLICE * half, SLICE), pl.ds(32 * again, 32)] = piece[:, 64:96]
+            main_op[op_rows, pl.ds(4 * SLICE + 64 * again, 64)] = piece[:, 0:64]
+            face_op[op_rows, pl.ds(32 * again, 32)] = piece[:, 64:96]
+    square = (SLICE, SLICE)
+    same = lax.broadcasted_iota(jnp.int32, square, 0) == lax.broadcasted_iota(jnp.int32, square, 1)
+    outer = jnp.where(span == 0, LIFT_HALF, -LIFT_HALF) * along - jnp.where(same, LIFT_HALF, 0.0)
+    edge_rows[pl.ds(0, SLICE), :] = edges
+    edge_rows[pl.ds(SLICE, 32), :] = jnp.zeros((32, LANES), jnp.float32)
+    lows = edge_rows[pl.ds(0, 32, stride=5), :][:, 0:32]
+    highs = edge_rows[pl.ds(4, 32, stride=5), :][:, 32:64]
+    pitch_op[...] = jnp.zeros_like(pitch_op)
+    for half in range(2):
+        for again in range(2):
+            span_op[pl.ds(SLICE * half, SLICE), pl.ds(SLICE * again, SLICE)] = halves(outer)[half]
+            pitch_op[pl.ds(32 * half, 32), pl.ds(32 * again, 32)] = halves(lows)[half]
+            pitch_op[pl.ds(64 + 32 * half, 32), pl.ds(64 + 32 * again, 32)] = halves(highs)[half]
 
     for copy in loads:
         copy.wait()
-    start_halo(0, 0)
-    for elem in (1, 2):
-        split_main(0, 0, elem)
+    span_copy(even, 0).start()
+    pack_up[0], pack_down[0] = packed(even)
+    for copy in pitch_copies(0):
+        copy.start()
 
     all_turned = pltpu.make_async_remote_copy(
         src_ref=turned.at[pl.ds(0, passes - 1)], dst_ref=turned.at[pl.ds(0, passes - 1)],
@@ -311,17 +354,15 @@
 
     lax.fori_loop(0, passes, rotate, 0, unroll=4)
 
-    wait_halo(0, 0)
-    for elem in (0, 3):
-        split_main(0, 0, elem)
-    split_ghosts(0, 0)
     for copy in old_loads:
         copy.wait()
 
     def store_residual(j, mine, part):
-        resid[j] = INV_DT * (mine - resid[j]) + part
-
-    apply(0, 0, store_residual)
+        at = pl.ds(SLICE * j, SLICE)
+        resid[at, :] = INV_DT * (mine - resid[at, :]) + part
+
+    apply(even, store_residual)
+    correct(resid, 0, 1.0, False)
 
     all_faced = pltpu.make_async_remote_copy(
         src_ref=facing, dst_ref=facing, send_sem=face_send, recv_sem=face_recv,
@@ -333,73 +374,70 @@
         block = jnp.concatenate([block, jnp.zeros((7, LANES), jnp.float32)], axis=0)
         for half, piece in enumerate(halves(block)):
             face_x[j // 4, pl.ds(32 * half, 32), pl.ds(LANES * (j % 4), LANES)] = piece
-    outs = [
-        pltpu.make_async_copy(resid.at[j, pl.ds(0, 125)], residual_out.at[:, j, 0, :], out_sem.at[0, j])
-        for j in range(SLICES)
-    ]
-    for s in range(5):
+    for s in (0, 4, 1, 2, 3):
         image = jnp.dot(face_op[...], face_x[s], preferred_element_type=jnp.float32)
         image = image[0:SLICE] + image[SLICE : 2 * SLICE]
         for elem in range(4):
-            j = 4 * s + elem
-            whole = resid[j] + image[:, LANES * elem : LANES * (elem + 1)]
-            resid[j] = whole
-            values[1, pl.ds(SLICE * j, SLICE), :] = whole * (-1.0 / DIAG)
-    for copy in outs:
+            at = pl.ds(SLICE * (4 * s + elem), SLICE)
+            whole = resid[at, :] + image[:, LANES * elem : LANES * (elem + 1)]
+            resid[at, :] = whole
+            odd[at, :] = whole * (-1.0 / DIAG)
+        if s == 4:
+            span_copy(odd, 1).start()
+    pack_up[1], pack_down[1] = packed(odd)
+    for copy in pitch_copies(1):
         copy.start()
 
+    def interleave(field, rows):
+        flat_rows = rows.reshape(125 * SLICES, LANES)
+        for j in range(SLICES):
+            flat_rows[pl.ds(j, 125, stride=SLICES), :] = field[pl.ds(SLICE * j, 125), :]
+
+    interleave(resid, resid_rows)
     rate = OMEGA / DIAG
-
-    def sweep(t, carry):
-        slot = lax.rem(t, 2)
-        start_halo(slot, t)
-        for elem in (1, 2):
-            split_main(slot, t, elem)
-        wait_halo(slot, t)
-        for elem in (0, 3):
-            split_main(slot, t, elem)
-        split_ghosts(slot, t)
+    for t in range(1, SWEEPS + 1):
+        field, after = values[t % 2], values[1 - t % 2]
 
         def store(j, mine, part):
+            at = pl.ds(SLICE * j, SLICE)
             image = (INV_DT + INV_DTAU) * mine + part
-            values[1 - slot, pl.ds(SLICE * j, SLICE), :] = mine - rate * (resid[j] + image)
-
-        apply(slot, t, store)
-        return carry
-
-    lax.fori_loop(1, SWEEPS + 1, sweep, 0)
-
-    last = (SWEEPS + 1) % 2
-    final = [
-        pltpu.make_async_copy(
-            values.at[last, pl.ds(SLICE * j, 125)], update_out.at[:, j, 0, :], out_sem.at[1, j]
-        )
-        for j in range(SLICES)
+            after[at, :] = mine - rate * (resid[at, :] + image)
+
+        apply(field, store)
+        correct(after, t, -rate, t < SWEEPS)
+    interleave(values[(SWEEPS + 1) % 2], update_rows)
+
+
+def write_kernel(resid, update, residual_out, update_out, sems):
+    copies = [
+        pltpu.make_async_copy(rows, out, sems.at[k])
+        for k, (rows, out) in enumerate(((update, update_out), (resid, residual_out)))
     ]
-    for copy in final:
+    for copy in copies:
         copy.start()
-    for copy in outs + final:
+    for copy in copies:
         copy.wait()
 
 
 def per_device(passes, state, old_state, jacobians, offset):
     shape = state.shape
     tile = TRACE // passes
-    anywhere = pl.BlockSpec(memory_space=pl.ANY)
     in_hbm = pl.BlockSpec(memory_space=pltpu.HBM)
     f32, bf16, dma = jnp.float32, jnp.bfloat16, pltpu.SemaphoreType.DMA
     exchanges = SWEEPS + 1
     viewed = (125, SLICES, 1, LANES)
     pinned = lambda x: pltpu.with_memory_space_constraint(x, pltpu.HBM)
-    outs = pl.pallas_call(
+    in_vmem = pl.BlockSpec(memory_space=pltpu.VMEM)
+    slices = (SLICE * SLICES + 40, LANES)
+    fields = pl.pallas_call(
         functools.partial(kernel, passes),
-        out_shape=[jax.ShapeDtypeStruct(viewed, f32)] * 2,
-        in_specs=[in_hbm, in_hbm, in_hbm,
-                  pl.BlockSpec(memory_space=pltpu.SMEM), in_hbm],
-        out_specs=[anywhere] * 2,
+        out_shape=[jax.ShapeDtypeStruct((625, 4, LANES), f32)] * 2,
+        in_specs=[in_hbm, in_hbm, in_hbm, pl.BlockSpec(memory_space=pltpu.SMEM), in_hbm],
+        out_specs=[in_vmem] * 2,
         scratch_shapes=[
-            pltpu.VMEM((2, SLICE * SLICES + 40, LANES), f32),
-            pltpu.VMEM((SLICES, SLICE, LANES), f32),
+            pltpu.VMEM(slices, f32),
+            pltpu.VMEM(slices, f32),
+            pltpu.VMEM(slices, f32),
             pltpu.VMEM((26, SLICES, 1, LANES), f32),
             pltpu.VMEM((passes, tile, LANES), f32),
             pltpu.VMEM((passes, tile, LANES), f32),
@@ -407,28 +445,38 @@
             pltpu.VMEM((13, SLICE, SLICE), f32),
             pltpu.VMEM((3, 8, LANES), f32),
             pltpu.VMEM((5, 3, 5), f32),
-            pltpu.VMEM((2 * SLICE, 4 * SLICE), bf16),
-            pltpu.VMEM((2 * SLICE, 128), bf16),
+            pltpu.VMEM((SLICE + 32, LANES), f32),
+            pltpu.VMEM((2 * SLICE, 5 * SLICE), bf16),
             pltpu.VMEM((2 * SLICE, 64), bf16),
-            pltpu.VMEM((5, 4 * SLICE, 4 * LANES), bf16),
-            pltpu.VMEM((5, 128, 4 * LANES), bf16),
+            pltpu.VMEM((2 * SLICE, 2 * SLICE), bf16),
+            pltpu.VMEM((128, 128), bf16),
+            pltpu.VMEM((5, 5 * SLICE, 4 * LANES), bf16),
             pltpu.VMEM((5, 64, 4 * LANES), bf16),
             pltpu.VMEM((exchanges, 32, LANES), f32),
             pltpu.VMEM((exchanges, 32, LANES), f32),
             pltpu.VMEM((exchanges, 32, LANES), f32),
             pltpu.VMEM((exchanges, 32, LANES), f32),
             pltpu.VMEM((exchanges, SLICE, LANES), f32),
-            dma((SLICES,)), dma((SLICES,)), dma((5,)), dma, dma, dma((2, SLICES)),
+            dma((SLICES,)), dma((SLICES,)), dma((5,)), dma, dma,
             dma, dma, dma, dma, dma((3, exchanges)), dma((3, exchanges)),
         ],
         compiler_params=pltpu.CompilerParams(
-            collective_id=0, has_side_effects=True, vmem_limit_bytes=48 * 1024 * 1024
+            collective_id=0, has_side_effects=True, vmem_limit_bytes=40 * 1024 * 1024
         ),
         name="pseudo_step",
     )(
         pinned(state.reshape(viewed)), pinned(old_state.reshape(viewed)),
         pinned(jnp.transpose(jacobians, (1, 0, 2))), offset, pinned(jnp.asarray(operator_patterns())),
     )
+    outs = pl.pallas_call(
+        write_kernel,
+        out_shape=[jax.ShapeDtypeStruct((625, 4, LANES), f32)] * 2,
+        in_specs=[pl.BlockSpec(memory_space=pl.ANY)] * 2,
+        out_specs=[in_hbm] * 2,
+        scratch_shapes=[dma((2,))],
+        compiler_params=pltpu.CompilerParams(vmem_limit_bytes=1024 * 1024),
+        name="write_fields",
+    )(*fields)
     return tuple(out.reshape(shape) for out in outs)
 
 

time: 57.2 us -> 49.3 us (0.86)
  Pallas kernels: 53.7 us -> 47.9 us
  local copies, waits for them, and re-layouts: 2.09 us -> 0 us
    pallas_call x1, Pallas kernels: 53.7 us -> 46.5 us  [per_device(): pl.pallas_call(functools.partial(kernel, passes), out_shape=[jax.ShapeDty...]
    unnamed x2 -> x0, local copies, waits for them, and re-layouts: 2.09 us -> none
    pallas_call x0 -> x1, Pallas kernels: none -> 1.49 us  [per_device(): pl.pallas_call(write_kernel, out_shape=[jax.ShapeDtypeStruct((625, 4, LAN...]
where the time goes in v3:
time: 49.3 us; the launch traced here: 49.2 us
  Pallas kernels  47.9 us (97%)
  between operations  1.28 us (3%)
    pallas_call x1, Pallas kernels, per_device(): pl.pallas_call(functools.partial(kernel, passes), out_shape=[jax.ShapeDty...  46.5 us
    pallas_call x1, Pallas kernels, per_device(): pl.pallas_call(write_kernel, out_shape=[jax.ShapeDtypeStruct((625, 4, LAN...  1.49 us

profile of v3, /device:TPU:2, one launch (start us, length us, event | category | flops | bytes accessed | tf_op | source)
XLA Modules:
  0.0 49.2 jit_solution(9117562843715292980)
XLA Ops:
  1.3 46.5 %pseudo_step.1 = (f32[625,4,128]{2,1,0:T(4,128)S(1)}, f32[625,4,128]{2,1,0:T(4,128)S(1)}) custom-call(f32[125,20,1,128]{3,2,1,0:T(1,128)} %bitcast.9, f32[125,20,1,128]{3,2,1,0:T(1,128)} %bitcast.10, f32[5,3,5]{2,1,0:T(4,128)} %bitcast.11, s32[1]{0:T(128)S(6)} %copy.9.offset, f32[13,128,128]{2,1,0:T(8,128)} %constant.2.clone.planes), custom_call_target="tpu_custom_call" | custom-call | tf_op jit(solution)/shard_map/pseudo_step/pallas_call | solution.py:432
  47.7 1.5 %write_fields.1 = (f32[625,4,128]{2,1,0:T(4,128)}, f32[625,4,128]{2,1,0:T(4,128)}) custom-call(f32[625,4,128]{2,1,0:T(4,128)S(1)} %get-tuple-element.6.resid, f32[625,4,128]{2,1,0:T(4,128)S(1)} %get-tuple-element.7.update), custom_call_target="tpu_custom_call" | custom-call | tf_op jit(solution)/shard_map/write_fields/pallas_call | solution.py:471

commit v4 on v3

--- a/solution.py
+++ b/solution.py
@@ -83,7 +83,7 @@
     main_op, face_op, span_op, pitch_op, main_x, face_x,
     pack_up, pack_down, from_low, from_high, from_span,
     load_sem, old_sem, trace_sem, pat_sem, jac_sem,
-    turn_send, turn_recv, face_send, face_recv, halo_send, halo_recv,
+    row_sem, turn_send, turn_recv, face_send, face_recv, halo_send, halo_recv,
 ):
     values = (even, odd)
     row, here, span = lax.axis_index("row"), lax.axis_index("pass"), lax.axis_index("span")
@@ -103,7 +103,6 @@
 
     def greet(step, carry):
         other = peer(step)
-        pl.semaphore_signal(barrier, inc=1, device_id=(1 - row, other, span), device_id_type=MESH)
         pl.semaphore_signal(barrier, inc=1, device_id=(row, other, span), device_id_type=MESH)
         return carry
 
@@ -264,7 +263,8 @@
     trace[pl.ds(25, 1)] = jnp.zeros((1, SLICES, 1, LANES), jnp.float32)
     for copy in trace_loads:
         copy.wait()
-    pl.semaphore_wait(barrier, 2 * passes)
+    pl.semaphore_wait(barrier, passes + 1)
+    pl.semaphore_signal(row_sem, inc=1, device_id=(1 - row, here, span), device_id_type=MESH)
     flat = trace.reshape(26 * SLICES, LANES)
 
     def turn_copy(other):
@@ -341,18 +341,23 @@
     within = lax.rem(shift, LANES)
     tile_lane = lax.broadcasted_iota(jnp.int32, (tile, LANES), 1)
 
-    def rotate(step, carry):
-        other = peer(step)
-        near = turned[lax.rem(other - places + passes, passes)]
-        far = turned[lax.rem(other - places + 2 * passes - 1, passes)]
-        ready[other] = pltpu.roll(jnp.where(tile_lane < LANES - within, near, far), within, 1)
-        pltpu.make_async_remote_copy(
-            src_ref=ready.at[other], dst_ref=facing.at[pl.ds(pl.multiple_of(tile * here, tile), tile)],
-            send_sem=face_send, recv_sem=face_recv, device_id=(1 - row, other, span), device_id_type=MESH,
-        ).start()
+    pl.semaphore_wait(row_sem, 1)
+    group = 16
+
+    def rotate(block, carry):
+        others = [peer(group * block + i) for i in range(group)]
+        for other in others:
+            near = turned[lax.rem(other - places + passes, passes)]
+            far = turned[lax.rem(other - places + 2 * passes - 1, passes)]
+            ready[other] = pltpu.roll(jnp.where(tile_lane < LANES - within, near, far), within, 1)
+        for other in others:
+            pltpu.make_async_remote_copy(
+                src_ref=ready.at[other], dst_ref=facing.at[pl.ds(pl.multiple_of(tile * here, tile), tile)],
+                send_sem=face_send, recv_sem=face_recv, device_id=(1 - row, other, span), device_id_type=MESH,
+            ).start()
         return carry
 
-    lax.fori_loop(0, passes, rotate, 0, unroll=4)
+    lax.fori_loop(0, passes // group, rotate, 0)
 
     for copy in old_loads:
         copy.wait()
@@ -458,7 +463,7 @@
             pltpu.VMEM((exchanges, 32, LANES), f32),
             pltpu.VMEM((exchanges, SLICE, LANES), f32),
             dma((SLICES,)), dma((SLICES,)), dma((5,)), dma, dma,
-            dma, dma, dma, dma, dma((3, exchanges)), dma((3, exchanges)),
+            pltpu.SemaphoreType.REGULAR, dma, dma, dma, dma, dma((3, exchanges)), dma((3, exchanges)),
         ],
         compiler_params=pltpu.CompilerParams(
             collective_id=0, has_side_effects=True, vmem_limit_bytes=40 * 1024 * 1024

time: 49.3 us -> 48 us (0.974)
  Pallas kernels: 47.9 us -> 46.6 us
    pallas_call x1, Pallas kernels: 46.5 us -> 45.1 us  [per_device(): pl.pallas_call(functools.partial(kernel, passes), out_shape=[jax.ShapeDty...]
where the time goes in v4:
time: 48 us; the launch traced here: 47.8 us
  Pallas kernels  46.6 us (97%)
  between operations  1.28 us (3%)
    pallas_call x1, Pallas kernels, per_device(): pl.pallas_call(functools.partial(kernel, passes), out_shape=[jax.ShapeDty...  45.1 us
    pallas_call x1, Pallas kernels, per_device(): pl.pallas_call(write_kernel, out_shape=[jax.ShapeDtypeStruct((625, 4, LAN...  1.49 us

profile of v4, /device:TPU:2, one launch (start us, length us, event | category | flops | bytes accessed | tf_op | source)
XLA Modules:
  0.0 47.8 jit_solution(9492227632588407720)
XLA Ops:
  1.3 45.1 %pseudo_step.1 = (f32[625,4,128]{2,1,0:T(4,128)S(1)}, f32[625,4,128]{2,1,0:T(4,128)S(1)}) custom-call(f32[125,20,1,128]{3,2,1,0:T(1,128)} %bitcast.9, f32[125,20,1,128]{3,2,1,0:T(1,128)} %bitcast.10, f32[5,3,5]{2,1,0:T(4,128)} %bitcast.11, s32[1]{0:T(128)S(6)} %copy.9.offset, f32[13,128,128]{2,1,0:T(8,128)} %constant.2.clone.planes), custom_call_target="tpu_custom_call" | custom-call | tf_op jit(solution)/shard_map/pseudo_step/pallas_call | solution.py:437
  46.4 1.5 %write_fields.1 = (f32[625,4,128]{2,1,0:T(4,128)}, f32[625,4,128]{2,1,0:T(4,128)}) custom-call(f32[625,4,128]{2,1,0:T(4,128)S(1)} %get-tuple-element.6.resid, f32[625,4,128]{2,1,0:T(4,128)S(1)} %get-tuple-element.7.update), custom_call_target="tpu_custom_call" | custom-call | tf_op jit(solution)/shard_map/write_fields/pallas_call | solution.py:476

commit v5 on v4

--- a/solution.py
+++ b/solution.py
@@ -69,6 +69,11 @@
     return planes
 
 
+def send_order():
+    far_z, far_y = (4, 3, 5, 2, 6, 1, 7, 0), (2, 1, 3, 0)
+    return [(y, z, core) for core in (1, 0) for z in far_z for y in far_y]
+
+
 def halves(x):
     high = x.astype(jnp.bfloat16)
     low = (x - high.astype(jnp.float32)).astype(jnp.bfloat16)
@@ -91,22 +96,17 @@
     tile = TRACE // passes
     deriv = gll_derivative()
 
-    def peer(step):
-        turn_z, turn_y, turn_core = step // 8, lax.rem(step // 2, 4), lax.rem(step + 1, 2)
-        along_z = 4 + (1 - 2 * lax.rem(turn_z, 2)) * ((turn_z + 1) // 2)
-        along_y = 2 + (1 - 2 * lax.rem(turn_y, 2)) * ((turn_y + 1) // 2)
-        y = lax.rem(here // 16 + along_y, 4)
-        z = lax.rem(here // 2 + along_z, 8)
-        return 16 * y + 2 * z + lax.rem(here + turn_core, 2)
+    order = send_order()
+
+    def at(offset):
+        y = lax.rem(here // 16 + offset[0], 4)
+        z = lax.rem(here // 2 + offset[1], 8)
+        return 16 * y + 2 * z + lax.rem(here + offset[2], 2)
 
     barrier = pltpu.get_barrier_semaphore()
 
-    def greet(step, carry):
-        other = peer(step)
-        pl.semaphore_signal(barrier, inc=1, device_id=(row, other, span), device_id_type=MESH)
-        return carry
-
-    lax.fori_loop(0, passes - 1, greet, 0)
+    for offset_of in order[:-1]:
+        pl.semaphore_signal(barrier, inc=1, device_id=(row, at(offset_of), span), device_id_type=MESH)
     pl.semaphore_signal(barrier, inc=1, device_id=(1 - row, here, span), device_id_type=MESH)
     pl.semaphore_signal(barrier, inc=1, device_id=(row, here, 1 - span), device_id_type=MESH)
 
@@ -272,11 +272,8 @@
             src_ref=flat.at[pl.ds(pl.multiple_of(tile * other, tile), tile)], dst_ref=turned.at[here],
             send_sem=turn_send, recv_sem=turn_recv, device_id=(row, other, span), device_id_type=MESH)
 
-    def turn(step, carry):
-        turn_copy(peer(step)).start()
-        return carry
-
-    lax.fori_loop(0, passes - 1, turn, 0)
+    for offset_of in order[:-1]:
+        turn_copy(at(offset_of)).start()
     turned[here] = flat[pl.ds(pl.multiple_of(tile * here, tile), tile), :]
 
     for field in (even, resid):
@@ -344,8 +341,8 @@
     pl.semaphore_wait(row_sem, 1)
     group = 16
 
-    def rotate(block, carry):
-        others = [peer(group * block + i) for i in range(group)]
+    def rotate(block):
+        others = [at(order[group * block + i]) for i in range(group)]
         for other in others:
             near = turned[lax.rem(other - places + passes, passes)]
             far = turned[lax.rem(other - places + 2 * passes - 1, passes)]
@@ -355,9 +352,9 @@
                 src_ref=ready.at[other], dst_ref=facing.at[pl.ds(pl.multiple_of(tile * here, tile), tile)],
                 send_sem=face_send, recv_sem=face_recv, device_id=(1 - row, other, span), device_id_type=MESH,
             ).start()
-        return carry
-
-    lax.fori_loop(0, passes // group, rotate, 0)
+
+    for block in range(passes // group):
+        rotate(block)
 
     for copy in old_loads:
         copy.wait()

time: 48 us -> 45.2 us (0.942)
  Pallas kernels: 46.6 us -> 43.8 us
    pallas_call x1, Pallas kernels: 45.1 us -> 42.3 us  [per_device(): pl.pallas_call(functools.partial(kernel, passes), out_shape=[jax.ShapeDty...]
where the time goes in v5:
time: 45.2 us; the launch traced here: 45.1 us
  Pallas kernels  43.8 us (97%)
  between operations  1.28 us (3%)
    pallas_call x1, Pallas kernels, per_device(): pl.pallas_call(functools.partial(kernel, passes), out_shape=[jax.ShapeDty...  42.3 us
    pallas_call x1, Pallas kernels, per_device(): pl.pallas_call(write_kernel, out_shape=[jax.ShapeDtypeStruct((625, 4, LAN...  1.49 us

profile of v5, /device:TPU:2, one launch (start us, length us, event | category | flops | bytes accessed | tf_op | source)
XLA Modules:
  0.0 45.1 jit_solution(1429028157642664558)
XLA Ops:
  1.3 42.3 %pseudo_step.1 = (f32[625,4,128]{2,1,0:T(4,128)S(1)}, f32[625,4,128]{2,1,0:T(4,128)S(1)}) custom-call(f32[125,20,1,128]{3,2,1,0:T(1,128)} %bitcast.9, f32[125,20,1,128]{3,2,1,0:T(1,128)} %bitcast.10, f32[5,3,5]{2,1,0:T(4,128)} %bitcast.11, s32[1]{0:T(128)S(6)} %copy.9.offset, f32[13,128,128]{2,1,0:T(8,128)} %constant.2.clone.planes), custom_call_target="tpu_custom_call" | custom-call | tf_op jit(solution)/shard_map/pseudo_step/pallas_call | solution.py:434
  43.6 1.5 %write_fields.1 = (f32[625,4,128]{2,1,0:T(4,128)}, f32[625,4,128]{2,1,0:T(4,128)}) custom-call(f32[625,4,128]{2,1,0:T(4,128)S(1)} %get-tuple-element.6.resid, f32[625,4,128]{2,1,0:T(4,128)S(1)} %get-tuple-element.7.update), custom_call_target="tpu_custom_call" | custom-call | tf_op jit(solution)/shard_map/write_fields/pallas_call | solution.py:473

commit v6 on v5

--- a/solution.py
+++ b/solution.py
@@ -367,7 +367,7 @@
     correct(resid, 0, 1.0, False)
 
     all_faced = pltpu.make_async_remote_copy(
-        src_ref=facing, dst_ref=facing, send_sem=face_send, recv_sem=face_recv,
+        src_ref=facing.at[pl.ds(0, TRACE)], dst_ref=facing.at[pl.ds(0, TRACE)], send_sem=face_send, recv_sem=face_recv,
         device_id=(1 - row, here, span), device_id_type=MESH)
     all_faced.wait()
 
@@ -393,7 +393,8 @@
     def interleave(field, rows):
         flat_rows = rows.reshape(125 * SLICES, LANES)
         for j in range(SLICES):
-            flat_rows[pl.ds(j, 125, stride=SLICES), :] = field[pl.ds(SLICE * j, 125), :]
+            flat_rows[pl.ds(j, 120, stride=SLICES), :] = field[pl.ds(SLICE * j, 120), :]
+            flat_rows[pl.ds(j + 117 * SLICES, 8, stride=SLICES), :] = field[pl.ds(SLICE * j + 117, 8), :]
 
     interleave(resid, resid_rows)
     rate = OMEGA / DIAG
@@ -443,7 +444,7 @@
             pltpu.VMEM((26, SLICES, 1, LANES), f32),
             pltpu.VMEM((passes, tile, LANES), f32),
             pltpu.VMEM((passes, tile, LANES), f32),
-            pltpu.VMEM((TRACE, LANES), f32),
+            pltpu.VMEM((TRACE + LANES, LANES), f32),
             pltpu.VMEM((13, SLICE, SLICE), f32),
             pltpu.VMEM((3, 8, LANES), f32),
             pltpu.VMEM((5, 3, 5), f32),

time: 45.2 us -> 45.2 us (level)
  no operation moved by 1% of the time
where the time goes in v6:
time: 45.2 us; the launch traced here: 45.1 us
  Pallas kernels  43.8 us (97%)
  between operations  1.28 us (3%)
    pallas_call x1, Pallas kernels, per_device(): pl.pallas_call(functools.partial(kernel, passes), out_shape=[jax.ShapeDty...  42.3 us
    pallas_call x1, Pallas kernels, per_device(): pl.pallas_call(write_kernel, out_shape=[jax.ShapeDtypeStruct((625, 4, LAN...  1.49 us

profile of v6, /device:TPU:2, one launch (start us, length us, event | category | flops | bytes accessed | tf_op | source)
XLA Modules:
  0.0 45.1 jit_solution(1449133247732001887)
XLA Ops:
  1.3 42.3 %pseudo_step.1 = (f32[625,4,128]{2,1,0:T(4,128)S(1)}, f32[625,4,128]{2,1,0:T(4,128)S(1)}) custom-call(f32[125,20,1,128]{3,2,1,0:T(1,128)} %bitcast.9, f32[125,20,1,128]{3,2,1,0:T(1,128)} %bitcast.10, f32[5,3,5]{2,1,0:T(4,128)} %bitcast.11, s32[1]{0:T(128)S(6)} %copy.9.offset, f32[13,128,128]{2,1,0:T(8,128)} %constant.2.clone.planes), custom_call_target="tpu_custom_call" | custom-call | tf_op jit(solution)/shard_map/pseudo_step/pallas_call | solution.py:435
  43.6 1.5 %write_fields.1 = (f32[625,4,128]{2,1,0:T(4,128)}, f32[625,4,128]{2,1,0:T(4,128)}) custom-call(f32[625,4,128]{2,1,0:T(4,128)S(1)} %get-tuple-element.6.resid, f32[625,4,128]{2,1,0:T(4,128)S(1)} %get-tuple-element.7.update), custom_call_target="tpu_custom_call" | custom-call | tf_op jit(solution)/shard_map/write_fields/pallas_call | solution.py:474

commit v7 on v6

--- a/solution.py
+++ b/solution.py
@@ -339,7 +339,7 @@
     tile_lane = lax.broadcasted_iota(jnp.int32, (tile, LANES), 1)
 
     pl.semaphore_wait(row_sem, 1)
-    group = 16
+    group = 8
 
     def rotate(block):
         others = [at(order[group * block + i]) for i in range(group)]
@@ -371,12 +371,12 @@
         device_id=(1 - row, here, span), device_id_type=MESH)
     all_faced.wait()
 
-    for j in range(SLICES):
-        block = facing[pl.ds(j, 25, stride=SLICES), :]
-        block = jnp.concatenate([block, jnp.zeros((7, LANES), jnp.float32)], axis=0)
-        for half, piece in enumerate(halves(block)):
-            face_x[j // 4, pl.ds(32 * half, 32), pl.ds(LANES * (j % 4), LANES)] = piece
     for s in (0, 4, 1, 2, 3):
+        for j in range(4 * s, 4 * s + 4):
+            block = facing[pl.ds(j, 25, stride=SLICES), :]
+            block = jnp.concatenate([block, jnp.zeros((7, LANES), jnp.float32)], axis=0)
+            for half, piece in enumerate(halves(block)):
+                face_x[j // 4, pl.ds(32 * half, 32), pl.ds(LANES * (j % 4), LANES)] = piece
         image = jnp.dot(face_op[...], face_x[s], preferred_element_type=jnp.float32)
         image = image[0:SLICE] + image[SLICE : 2 * SLICE]
         for elem in range(4):

time: 45.2 us -> 45.1 us (level)
  no operation moved by 1% of the time
where the time goes in v7:
time: 45.1 us; the launch traced here: 45 us
  Pallas kernels  43.7 us (97%)
  between operations  1.28 us (3%)
    pallas_call x1, Pallas kernels, per_device(): pl.pallas_call(functools.partial(kernel, passes), out_shape=[jax.ShapeDty...  42.2 us
    pallas_call x1, Pallas kernels, per_device(): pl.pallas_call(write_kernel, out_shape=[jax.ShapeDtypeStruct((625, 4, LAN...  1.49 us

profile of v7, /device:TPU:2, one launch (start us, length us, event | category | flops | bytes accessed | tf_op | source)
XLA Modules:
  0.0 45.0 jit_solution(8393624039468548126)
XLA Ops:
  1.3 42.2 %pseudo_step.1 = (f32[625,4,128]{2,1,0:T(4,128)S(1)}, f32[625,4,128]{2,1,0:T(4,128)S(1)}) custom-call(f32[125,20,1,128]{3,2,1,0:T(1,128)} %bitcast.9, f32[125,20,1,128]{3,2,1,0:T(1,128)} %bitcast.10, f32[5,3,5]{2,1,0:T(4,128)} %bitcast.11, s32[1]{0:T(128)S(6)} %copy.9.offset, f32[13,128,128]{2,1,0:T(8,128)} %constant.2.clone.planes), custom_call_target="tpu_custom_call" | custom-call | tf_op jit(solution)/shard_map/pseudo_step/pallas_call | solution.py:435
  43.5 1.5 %write_fields.1 = (f32[625,4,128]{2,1,0:T(4,128)}, f32[625,4,128]{2,1,0:T(4,128)}) custom-call(f32[625,4,128]{2,1,0:T(4,128)S(1)} %get-tuple-element.6.resid, f32[625,4,128]{2,1,0:T(4,128)S(1)} %get-tuple-element.7.update), custom_call_target="tpu_custom_call" | custom-call | tf_op jit(solution)/shard_map/write_fields/pallas_call | solution.py:474
